TPU v7x, 1024 devices: a whole 8x8x8 slice. The times are simulated.
1024 devices in a mesh: node: 256 (over x, z_lo, y), local: 4 (over z_hi, core).
Axes of the slice: x: 8, y: 8, z: 8 (z_hi: 2, z_lo: 4; z = z_hi * 4 + z_lo), core: 2. Of those that a mesh axis runs over, the one named last changes fastest.
Arguments:
- x_groups: bfloat16 [65536, 2560], P('node'), may hold values from -6 to 6
- group_len: int32 [256, 4, 2], replicated, may hold values from 10 to 32, as said below
- act_grad: bfloat16 [65536, 1024], P('node', 'local'), may hold values from -24 to 24
- slot_gate: bfloat16 [65536], P('node'), may hold values from 0.099609375 to 1
- gate_up: bfloat16 [256, 2560, 1024], P('node', None, 'local'), may hold values from -0.125 to 0.125
Outputs:
- grad_rows: bfloat16 [65536, 2560], P(('node', 'local'))
- grad_gate_up: bfloat16 [256, 2560, 1024], P('node', None, 'local')
Inputs may be any that keep to these rules, and one draw needn't show every extreme that they name: `group_len`: in each of the two groups some device has all 32 slots live.
All inputs are finite; a program needn't handle non-finite values.
Results may differ from a plain program's by a relative error of at most 0.015.
Values may be sent and summed in bfloat16 or wider, within the bound.
No kernel may reach another device: no remote copies, remote signals or barrier semaphores. Data moves between devices by JAX's collectives and lax.ppermute only.
A program may use at most 32 MiB of HBM per device.

v0:
```python
import math

import jax
import jax.numpy as jnp
from jax import lax
from jax.sharding import PartitionSpec as P


def from_behind(value, axis, steps):
    count = lax.axis_size(axis)
    pairs = [(source, (source + steps) % count) for source in range(count)]
    return lax.ppermute(value, axis, pairs)


def swapped(block, axis, bit):
    count = lax.axis_size(axis)
    route = []
    for low in range(count):
        high = low | 1 << bit
        if high != low and high < count:
            route += [(low, high), (high, low)]
    return lax.ppermute(block, axis, route)


def expert_work(slot_rows, cotangents, gate_values, weights, factor):
    column_half = weights.shape[1] // 2
    hidden = jnp.dot(slot_rows, weights, preferred_element_type=jnp.float32)
    gate_part = hidden[:, :column_half]
    up_part = hidden[:, column_half:]
    weighted = gate_values.astype(jnp.float32)[:, None] * cotangents.astype(jnp.float32)
    sigmoid_g = jax.nn.sigmoid(gate_part)
    d_gate = weighted * up_part * sigmoid_g * (1.0 + gate_part * (1.0 - sigmoid_g))
    d_up = weighted * gate_part * sigmoid_g
    d_hidden = jnp.concatenate([d_gate, d_up], axis=1).astype(jnp.bfloat16)
    partial_value = lax.dot_general(
        d_hidden, weights, (((1,), (1,)), ((), ())), preferred_element_type=jnp.float32
    )
    term = (
        lax.dot_general(
            slot_rows, d_hidden, (((0,), (0,)), ((), ())), preferred_element_type=jnp.float32
        )
        * factor
    )
    return (partial_value, term)


def on_device(x_groups, group_len, act_grad, slot_gate, gate_up):
    node_rows, row_width = x_groups.shape
    in_node = lax.axis_size("local")
    slot_count = node_rows // (2 * in_node)
    column_half = gate_up.shape[2] // 2
    node_at = lax.axis_index("node")
    local_at = lax.axis_index("local")
    parity = node_at % 2
    factor = 1.0 / math.sqrt(4 * in_node * slot_count)
    weights = gate_up[0]
    lengths = lax.dynamic_index_in_dim(group_len, node_at, 0, keepdims=False)
    alive = jnp.arange(slot_count)[None, None, :] < lengths[:, :, None]
    shaped_rows = x_groups.reshape(in_node, 2, slot_count, row_width)
    shaped_rows = jnp.where(alive[:, :, :, None], shaped_rows, jnp.zeros_like(shaped_rows))
    shaped_cot = act_grad.reshape(in_node, 2, slot_count, 2 * column_half)
    shaped_gate = slot_gate.reshape(in_node, 2, slot_count)
    next_weights = from_behind(weights, "node", -2)
    flat_rows = shaped_rows.reshape(node_rows, row_width)
    flat_cot = shaped_cot.reshape(node_rows, 2 * column_half)
    flat_gate = shaped_gate.reshape(node_rows)
    mine_cols = lax.dynamic_slice_in_dim(flat_cot, parity * column_half, column_half, 1)
    other_cols = lax.dynamic_slice_in_dim(flat_cot, (1 - parity) * column_half, column_half, 1)
    partner = swapped((flat_rows, other_cols, flat_gate), "node", 0)
    pair_rows = jnp.concatenate([flat_rows, partner[0]], axis=0).reshape(
        2, in_node, 2, slot_count, row_width
    )
    pair_cot = jnp.concatenate([mine_cols, partner[1]], axis=0).reshape(
        2, in_node, 2, slot_count, column_half
    )
    pair_gate = jnp.concatenate([flat_gate, partner[2]], axis=0).reshape(2, in_node, 2, slot_count)
    first_partial, first_term = expert_work(
        pair_rows[:, :, 0].reshape(-1, row_width),
        pair_cot[:, :, 0].reshape(-1, column_half),
        pair_gate[:, :, 0].reshape(-1),
        weights,
        factor,
    )
    second_partial, second_term = expert_work(
        pair_rows[:, :, 1].reshape(-1, row_width),
        pair_cot[:, :, 1].reshape(-1, column_half),
        pair_gate[:, :, 1].reshape(-1),
        next_weights,
        factor,
    )
    stacked = jnp.stack(
        [
            first_partial.reshape(2, in_node, slot_count, row_width),
            second_partial.reshape(2, in_node, slot_count, row_width),
        ],
        axis=2,
    )
    stacked = stacked.reshape(2, in_node, 2 * slot_count, row_width)
    summed = lax.psum_scatter(
        stacked.astype(jnp.bfloat16), "local", scatter_dimension=1, tiled=True
    ).astype(jnp.float32)
    returned = swapped(summed[1].astype(jnp.bfloat16), "node", 0).astype(jnp.float32)
    combined = (summed[0] + returned)[0]
    finished = combined.astype(jnp.bfloat16)
    carried = from_behind(second_term.astype(jnp.bfloat16), "node", 2)
    grad_weights = (first_term + carried.astype(jnp.float32)).astype(jnp.bfloat16)
    mine_alive = lax.dynamic_index_in_dim(alive, local_at, 0, keepdims=False).reshape(-1)
    grad_rows = jnp.where(mine_alive[:, None], finished, jnp.zeros_like(finished))
    return (grad_rows, grad_weights[None])


def solution(mesh):
    placed = (P("node", None), P(), P("node", "local"), P("node"), P("node", None, "local"))
    return jax.shard_map(
        on_device,
        mesh=mesh,
        in_specs=placed,
        out_specs=(P(("node", "local"), None), P("node", None, "local")),
        check_vma=False,
    )
```

profile of v0, /device:TPU:14, one launch (start us, length us, event | category | flops | bytes accessed | tf_op | source)
XLA Modules:
  0.0 295.0 jit_solution(16162133236722881551)
XLA Ops:
  7.2 0.0 copy-start
  7.2 0.0 all-reduce.3.cloned.1.call-start
  7.2 0.6 copy-done
  7.9 0.1 constant_dynamic-slice_fusion.3
  7.9 0.1 copy.20
  8.0 0.1 copy.21
  8.1 0.1 iota_compare_fusion
  8.2 0.1 lt.51
  8.3 0.0 copy-start.1
  8.3 0.0 copy-start.2
  8.3 1.5 broadcast_select_fusion
  9.8 3.6 %collective-permute-start.2 = (bf16[256,2560]{1,0:T(8,128)(2,1)S(1)}, bf16[256,2560]{1,0:T(8,128)(2,1)S(1)}, u32[]{:S(2)}, u32[]{:S(2)}) collective-permute-start(bf16[256,2560]{1,0:T(8,128)(2,1)S(1)} %broadcast_select_fusion), channel_id=1, source_target_pairs={{0,4},{4,0},{8,12},{12,8},{16,20},{20,16},{24,28},{28,24},{32,36},... | collective-permute-start | bytes 3932168 | tf_op jit(solution)/shard_map/ppermute | solution.py:22
  13.5 0.0 copy-done.1
  13.5 2.2 collective-permute-start.1
  15.7 15.9 %collective-permute-start.3 = (bf16[2560,256]{1,0:T(8,128)(2,1)}, bf16[2560,256]{1,0:T(8,128)(2,1)}, u32[]{:S(2)}, u32[]{:S(2)}) collective-permute-start(bf16[2560,256]{1,0:T(8,128)(2,1)} %bitcast.5), channel_id=1, source_target_pairs={{0,1016},{4,1020},{8,0},{12,4},{16,8},{20,12},{24,16},{28,20},{32,... | collective-permute-start | bytes 3932168 | tf_op jit(solution)/shard_map/ppermute | solution.py:12
  31.6 0.0 copy-done.2
  31.6 2.7 collective-permute-start
  34.3 0.1 concatenate.33
  34.4 65.5 %collective-permute-done = bf16[256]{0:T(256)(128)(2,1)S(1)} collective-permute-done((bf16[256]{0:T(256)(128)(2,1)S(1)}, bf16[256]{0:T(256)(128)(2,1)S(1)}, u32[]{:S(2)}, u32[]{:S(2)}) %collective-permute-start) | collective-permute-done | bytes 544 | tf_op jit(solution)/shard_map/ppermute | solution.py:22
  99.9 0.1 concatenate.34
  100.0 0.1 reshape.85
  100.1 0.1 reshape.83
  100.2 0.0 collective-permute-done.1
  100.2 0.0 collective-permute-done.2
  100.2 0.2 pad_maximum_fusion
  100.4 0.2 fusion.33
  100.6 1.8 fusion.31
  102.5 0.1 fusion.12
  102.6 1.9 fusion.1
  104.5 0.0 collective-permute-done.3
  104.5 1.8 fusion.35
  106.3 0.1 fusion.9
  106.4 1.9 convolution_convert_fusion
  108.3 0.2 pad_maximum_fusion.1
  108.5 1.7 copy.26
  110.2 0.0 all-reduce.3.cloned.1.call-update
  110.2 1.6 fusion
  111.9 4.6 %collective-permute-start.5 = (bf16[2560,256]{1,0:T(8,128)(2,1)}, bf16[2560,256]{1,0:T(8,128)(2,1)}, u32[]{:S(2)}, u32[]{:S(2)}) collective-permute-start(bf16[2560,256]{1,0:T(8,128)(2,1)} %fusion), channel_id=1, source_target_pairs={{0,8},{4,12},{8,16},{12,20},{16,24},{20,28},{24,32},{28,36},{32,40... | collective-permute-start | bytes 3932168 | tf_op jit(solution)/shard_map/ppermute | solution.py:12
  116.5 1.3 dynamic-slice
  117.8 154.6 %all-reduce.3.cloned.1.call-done = bf16[2,4,64,2560]{3,2,1,0:T(8,128)(2,1)} async-done(((bf16[2,4,64,2560]{3,2,1,0:T(8,128)(2,1)}), bf16[2,4,64,2560]{3,2,1,0:T(8,128)(2,1)}) %all-reduce.3.cloned.1.call-update) | async-done | bytes 2621456
  272.5 1.6 dynamic-slice_bitcast_fusion
  274.1 3.4 %collective-permute-start.4 = (bf16[1,64,2560]{2,1,0:T(8,128)(2,1)S(1)}, bf16[1,64,2560]{2,1,0:T(8,128)(2,1)S(1)}, u32[]{:S(2)}, u32[]{:S(2)}) collective-permute-start(bf16[1,64,2560]{2,1,0:T(8,128)(2,1)S(1)} %dynamic-slice_bitcast_fusion), channel_id=1, source_target_pairs={{0,4},{4,0},{8,12},{12,8},{16,20},{20,16},{24,28},{28,24},{32,36},... | collective-permute-start | bytes 983048 | tf_op jit(solution)/shard_map/ppermute | solution.py:22
  277.5 0.1 broadcast_in_dim.32
  277.6 0.0 collective-permute-done.5
  277.6 2.9 fusion.2
  280.5 5.2 %collective-permute-done.4 = bf16[1,64,2560]{2,1,0:T(8,128)(2,1)S(1)} collective-permute-done((bf16[1,64,2560]{2,1,0:T(8,128)(2,1)S(1)}, bf16[1,64,2560]{2,1,0:T(8,128)(2,1)S(1)}, u32[]{:S(2)}, u32[]{:S(2)}) %collective-permute-start.4) | collective-permute-done | bytes 327712 | tf_op jit(solution)/shard_map/ppermute | solution.py:22
  285.7 2.4 fusion.6
  (7 shorter events, 0.1 us)
Async XLA Ops:
  7.2 0.7 copy-start
  7.2 265.3 %all-reduce.3.cloned.1.call-start = ((), (), s32[]{:S(2)}) async-start(), calls=%async_computation | async-start | bytes 5242880
  8.3 5.1 %copy-start.1 = (bf16[256,256]{1,0:T(8,128)(2,1)S(1)}, bf16[256,256]{1,0:T(8,128)(2,1)}, u32[]{:S(2)}) copy-start(bf16[256,256]{1,0:T(8,128)(2,1)} %param.7) | copy-start | bytes 393220
  8.3 23.3 %copy-start.2 = (bf16[256]{0:T(256)(128)(2,1)S(1)}, bf16[256]{0:T(256)(128)(2,1)}, u32[]{:S(2)}) copy-start(bf16[256]{0:T(256)(128)(2,1)} %param.8) | copy-start | bytes 1540
  9.8 90.4 %collective-permute-start.2 = (bf16[256,2560]{1,0:T(8,128)(2,1)S(1)}, bf16[256,2560]{1,0:T(8,128)(2,1)S(1)}, u32[]{:S(2)}, u32[]{:S(2)}) collective-permute-start(bf16[256,2560]{1,0:T(8,128)(2,1)S(1)} %broadcast_select_fusion), channel_id=1, source_target_pairs={{0,4},{4,0},{8,12},{12,8},{16,20},{20,16},{24,28},{28,24},{32,36},... | collective-permute-start | bytes 3932168 | tf_op jit(solution)/shard_map/ppermute | solution.py:22
  13.5 86.7 %collective-permute-start.1 = (bf16[256,128]{1,0:T(8,128)(2,1)S(1)}, bf16[256,128]{1,0:T(8,128)(2,1)S(1)}, u32[]{:S(2)}, u32[]{:S(2)}) collective-permute-start(bf16[256,128]{1,0:T(8,128)(2,1)S(1)} %get-tuple-element.13), channel_id=1, source_target_pairs={{0,4},{4,0},{8,12},{12,8},{16,20},{20,16},{24,28},{28,24},{32,36},... | collective-permute-start | bytes 196616 | tf_op jit(solution)/shard_map/ppermute | solution.py:22
  15.7 88.7 %collective-permute-start.3 = (bf16[2560,256]{1,0:T(8,128)(2,1)}, bf16[2560,256]{1,0:T(8,128)(2,1)}, u32[]{:S(2)}, u32[]{:S(2)}) collective-permute-start(bf16[2560,256]{1,0:T(8,128)(2,1)} %bitcast.5), channel_id=1, source_target_pairs={{0,1016},{4,1020},{8,0},{12,4},{16,8},{20,12},{24,16},{28,20},{32,... | collective-permute-start | bytes 3932168 | tf_op jit(solution)/shard_map/ppermute | solution.py:12
  31.6 68.3 %collective-permute-start = (bf16[256]{0:T(256)(128)(2,1)S(1)}, bf16[256]{0:T(256)(128)(2,1)S(1)}, u32[]{:S(2)}, u32[]{:S(2)}) collective-permute-start(bf16[256]{0:T(256)(128)(2,1)S(1)} %copy-done.2), channel_id=1, source_target_pairs={{0,4},{4,0},{8,12},{12,8},{16,20},{20,16},{24,28},{28,24},{32,36},... | collective-permute-start | bytes 1544 | tf_op jit(solution)/shard_map/ppermute | solution.py:22
  111.9 165.8 %collective-permute-start.5 = (bf16[2560,256]{1,0:T(8,128)(2,1)}, bf16[2560,256]{1,0:T(8,128)(2,1)}, u32[]{:S(2)}, u32[]{:S(2)}) collective-permute-start(bf16[2560,256]{1,0:T(8,128)(2,1)} %fusion), channel_id=1, source_target_pairs={{0,8},{4,12},{8,16},{12,20},{16,24},{20,28},{24,32},{28,36},{32,40... | collective-permute-start | bytes 3932168 | tf_op jit(solution)/shard_map/ppermute | solution.py:12
  274.1 11.7 %collective-permute-start.4 = (bf16[1,64,2560]{2,1,0:T(8,128)(2,1)S(1)}, bf16[1,64,2560]{2,1,0:T(8,128)(2,1)S(1)}, u32[]{:S(2)}, u32[]{:S(2)}) collective-permute-start(bf16[1,64,2560]{2,1,0:T(8,128)(2,1)S(1)} %dynamic-slice_bitcast_fusion), channel_id=1, source_target_pairs={{0,4},{4,0},{8,12},{12,8},{16,20},{20,16},{24,28},{28,24},{32,36},... | collective-permute-start | bytes 983048 | tf_op jit(solution)/shard_map/ppermute | solution.py:22
Sparse Core Ops, SparseCore 0:
  110.4 162.0 all-reduce.2
where the time goes:
time: 296 us; the launch traced here: 295 us
  waiting for transfers between devices  225 us (76%)
  starting transfers between devices  32.5 us (11%)
  between operations  14.3 us (5%)
  matrix products  11.9 us (4%)
  local copies, waits for them, and re-layouts  6.32 us (2%)
  other arithmetic  4.72 us (2%)
    unnamed x2, waiting for transfers between devices  155 us
    ppermute x4, waiting for transfers between devices, swapped(): return lax.ppermute(block, axis, route)  70.7 us
    ppermute x2, starting transfers between devices, from_behind(): return lax.ppermute(value, axis, pairs)  20.5 us
    ppermute x4, starting transfers between devices, swapped(): return lax.ppermute(block, axis, route)  12 us
  transfers between devices with their start and end apart: 7, of which 3 were waited for; matrix products, arithmetic and copies ran while one was open for 4% of the time, Pallas kernels for 0%

commit v1 on v0

v1 whole, which is shorter than its diff:
```python
import math

import jax
import jax.numpy as jnp
from jax import lax
from jax.sharding import PartitionSpec as P

BF = jnp.bfloat16
F32 = jnp.float32


def ahead(value, steps):
    count = lax.axis_size("node")
    return lax.ppermute(value, "node", [(i, (i + steps) % count) for i in range(count)])


def swapped(value, axis, bit):
    count = lax.axis_size(axis)
    return lax.ppermute(value, axis, [(i, i ^ (1 << bit)) for i in range(count)])


def pick(array, index, axis):
    return lax.dynamic_index_in_dim(array, index, axis, keepdims=False)


def hidden_grads(rows, cot, weights, width):
    hidden = jnp.dot(rows, weights, preferred_element_type=F32)
    parts = []
    for k in range(2):
        gate = hidden[:, 2 * k * width : (2 * k + 1) * width]
        up = hidden[:, (2 * k + 1) * width : (2 * k + 2) * width]
        c = cot[:, k * width : (k + 1) * width].astype(F32)
        s = jax.nn.sigmoid(gate)
        parts += [c * up * s * (1.0 + gate * (1.0 - s)), c * gate * s]
    return jnp.concatenate(parts, axis=1).astype(BF)


def row_grads(dh, weights):
    return lax.dot_general(dh, weights, (((1,), (1,)), ((), ())), preferred_element_type=F32)


def weight_grads(rows, dh):
    return lax.dot_general(rows, dh, (((0,), (0,)), ((), ())), preferred_element_type=F32)


def on_device(x_groups, group_len, act_grad, slot_gate, gate_up):
    node_rows, dim = x_groups.shape
    in_node = lax.axis_size("local")
    cap = node_rows // (2 * in_node)
    width = gate_up.shape[2] // 2
    half = in_node // 2 * cap
    node = lax.axis_index("node")
    local = lax.axis_index("local")
    core = local % 2
    far = local // 2
    parity = node % 2
    factor = 1.0 / math.sqrt(4 * in_node * cap)

    own_w = gate_up[0]
    acts = act_grad.reshape(in_node // 2, 2, 2, cap, 2 * width)
    act_other = swapped(pick(acts, 1 - core, 1), "local", 0)
    act_mine = pick(acts, core, 1)
    both_w = jnp.concatenate([own_w, swapped(own_w, "local", 0)], axis=1)

    lengths = pick(group_len, node, 0)
    alive = jnp.arange(cap)[None, None, :] < lengths[:, :, None]
    alive_half = pick(alive.reshape(in_node // 2, 2, 2, cap), core, 1)
    rows = pick(x_groups.reshape(in_node // 2, 2, 2, cap, dim), core, 1)
    rows = jnp.where(alive_half[..., None], rows, jnp.zeros_like(rows))
    gates = pick(slot_gate.reshape(in_node // 2, 2, 2, cap), core, 1).astype(F32)

    def cots(which):
        cut = [
            pick(a.reshape(in_node // 2, 2, cap, 2, width), which, 3) for a in (act_mine, act_other)
        ]
        both = jnp.concatenate(cut, axis=-1).astype(F32)
        return (both * gates[..., None]).astype(BF)

    keep = cots(parity)
    give = cots(1 - parity)

    def group(array, k):
        return array[:, k].reshape(half, array.shape[-1])

    sent1 = ahead(jnp.concatenate([group(rows, 1), group(give, 1), group(keep, 1)], axis=1), 2)
    sent0 = jnp.concatenate([group(rows, 0), group(give, 0)], axis=1)
    got0 = swapped(sent0, "node", 0)
    got1 = swapped(sent1[:, : dim + 2 * width], "node", 0)

    rows0 = jnp.concatenate([group(rows, 0), got0[:, :dim]], axis=0)
    cot0 = jnp.concatenate([group(keep, 0), got0[:, dim:]], axis=0)
    rows1 = jnp.concatenate([sent1[:, :dim], got1[:, :dim]], axis=0)
    cot1 = jnp.concatenate([sent1[:, dim + 2 * width :], got1[:, dim:]], axis=0)

    def summed(dx):
        own = dx[:half] + swapped(dx[half:].astype(BF), "node", 0).astype(F32)
        own = own.reshape(2, cap, dim)
        away = swapped(pick(own, 1 - far, 0).astype(BF), "local", 1).astype(F32)
        return (pick(own, far, 0) + away).astype(BF)

    dh0 = hidden_grads(rows0, cot0, both_w, width)
    out0 = summed(row_grads(dh0, both_w))
    dh1 = hidden_grads(rows1, cot1, both_w, width)
    out1 = ahead(summed(row_grads(dh1, both_w)), -2)

    all_rows = jnp.concatenate([rows0, rows1], axis=0)
    all_dh = jnp.concatenate([dh0, dh1], axis=0)
    other_dw = (weight_grads(all_rows, all_dh[:, 2 * width :]) * factor).astype(BF)
    other_dw = swapped(other_dw, "local", 0)
    own_dw = weight_grads(all_rows, all_dh[:, : 2 * width]) * factor
    grad_weights = (own_dw + other_dw.astype(F32)).astype(BF)

    mine = pick(alive, local, 0)
    finished = jnp.stack([out0, out1], axis=0)
    finished = jnp.where(mine[:, :, None], finished, jnp.zeros_like(finished))
    return (finished.reshape(2 * cap, dim), grad_weights[None])


def solution(mesh):
    placed = (P("node", None), P(), P("node", "local"), P("node"), P("node", None, "local"))
    return jax.shard_map(
        on_device,
        mesh=mesh,
        in_specs=placed,
        out_specs=(P(("node", "local"), None), P("node", None, "local")),
        check_vma=False,
    )
```

time: 296 us -> 107 us (0.36)
  waiting for transfers between devices: 225 us -> 37.4 us
  starting transfers between devices: 32.5 us -> 50.7 us
  between operations: 14.3 us -> 1.15 us
  other arithmetic: 4.72 us -> 1.74 us
    unnamed x2 -> x0, waiting for transfers between devices: 155 us -> none
    ppermute x6 -> x11, waiting for transfers between devices: 70.7 us -> 37.4 us  [the longest x2 27.6 us: ahead(): lax.ppermute(value, 'node', [(i, (i + steps) % count) for i in range(coun...]
    ppermute x6 -> x11, starting transfers between devices: 32.5 us -> 50.7 us  [the longest x9 35.8 us: swapped(): return lax.ppermute(value, axis, [(i, i ^ 1 << bit) for i in range(count)])]
  transfers between devices with their start and end apart: 7 -> 11, of which waited for: 3 -> 5; matrix products, arithmetic and copies ran while one was open for 4% -> 8% of each run, Pallas kernels for 0% -> 0%
where the time goes in v1:
time: 107 us; the launch traced here: 105 us
  starting transfers between devices  50.7 us (47%)
  waiting for transfers between devices  37.4 us (35%)
  matrix products  10.4 us (10%)
  local copies, waits for them, and re-layouts  3.64 us (3%)
  other arithmetic  1.74 us (2%)
  between operations  1.15 us (1%)
    ppermute x9, starting transfers between devices, swapped(): return lax.ppermute(value, axis, [(i, i ^ 1 << bit) for i in range(count)])  35.8 us
    ppermute x2, waiting for transfers between devices, ahead(): lax.ppermute(value, 'node', [(i, (i + steps) % count) for i in range(coun...  27.6 us
    ppermute x2, starting transfers between devices, ahead(): lax.ppermute(value, 'node', [(i, (i + steps) % count) for i in range(coun...  15 us
    ppermute x9, waiting for transfers between devices, swapped(): return lax.ppermute(value, axis, [(i, i ^ 1 << bit) for i in range(count)])  9.77 us
    dot_general x2, matrix products, row_grads(): lax.dot_general(dh, weights, (((1,), (1,)), ((), ())), preferred_element_...  4.57 us
    dot_general x2, matrix products, hidden_grads(): hidden = jnp.dot(rows, weights, preferred_element_type=F32)  3.65 us
    dot_general x2, matrix products, weight_grads(): lax.dot_general(rows, dh, (((0,), (0,)), ((), ())), preferred_element_typ...  2.18 us
  transfers between devices with their start and end apart: 11, of which 5 were waited for; matrix products, arithmetic and copies ran while one was open for 8% of the time, Pallas kernels for 0%

profile of v1, /device:TPU:14, one launch (start us, length us, event | category | flops | bytes accessed | tf_op | source)
XLA Modules:
  0.0 105.1 jit_solution(16987766003556665732)
XLA Ops:
  0.6 0.0 copy-start
  0.7 1.0 dynamic-slice_bitcast_fusion.1
  1.7 1.9 %collective-permute-start = (bf16[2,2,32,256]{3,2,1,0:T(8,128)(2,1)S(1)}, bf16[2,2,32,256]{3,2,1,0:T(8,128)(2,1)S(1)}, u32[]{:S(2)}, u32[]{:S(2)}) collective-permute-start(bf16[2,2,32,256]{3,2,1,0:T(8,128)(2,1)S(1)} %get-tuple-element.15), channel_id=1, source_target_pairs={{0,1},{1,0},{2,3},{3,2},{4,5},{5,4},{6,7},{7,6},{8,9},{9,8},{10,11... | collective-permute-start | bytes 196616 | tf_op jit(solution)/shard_map/ppermute | solution.py:19
  3.6 2.4 %collective-permute-start.2 = (bf16[2560,256]{1,0:T(8,128)(2,1)}, bf16[2560,256]{1,0:T(8,128)(2,1)}, u32[]{:S(2)}, u32[]{:S(2)}) collective-permute-start(bf16[2560,256]{1,0:T(8,128)(2,1)} %bitcast.87), channel_id=1, source_target_pairs={{0,1},{1,0},{2,3},{3,2},{4,5},{5,4},{6,7},{7,6},{8,9},{9,8},{10,11... | collective-permute-start | bytes 3932168 | tf_op jit(solution)/shard_map/ppermute | solution.py:19
  6.0 0.7 reshape.53
  6.8 0.9 fusion.65
  7.7 0.1 compare_bitcast_fusion
  7.8 0.0 copy-done
  7.8 0.2 bitcast_select_fusion
  8.1 0.0 collective-permute-done
  8.1 0.3 constant_dynamic-slice_fusion
  8.5 0.1 multiply_convert_fusion
  8.7 4.7 %collective-permute-start.5 = (bf16[64,3072]{1,0:T(8,128)(2,1)S(1)}, bf16[64,3072]{1,0:T(8,128)(2,1)S(1)}, u32[]{:S(2)}, u32[]{:S(2)}) collective-permute-start(bf16[64,3072]{1,0:T(8,128)(2,1)S(1)} %pad_maximum_fusion.2), channel_id=1, source_target_pairs={{0,8},{4,12},{8,16},{12,20},{16,24},{20,28},{24,32},{28,36},{32,40... | collective-permute-start | bytes 1179656 | tf_op jit(solution)/shard_map/ppermute | solution.py:14
  13.4 3.6 %collective-permute-start.1 = (bf16[64,2816]{1,0:T(8,128)(2,1)S(1)}, bf16[64,2816]{1,0:T(8,128)(2,1)S(1)}, u32[]{:S(2)}, u32[]{:S(2)}) collective-permute-start(bf16[64,2816]{1,0:T(8,128)(2,1)S(1)} %pad_maximum_fusion.3), channel_id=1, source_target_pairs={{0,4},{4,0},{8,12},{12,8},{16,20},{20,16},{24,28},{28,24},{32,36},... | collective-permute-start | bytes 1081352 | tf_op jit(solution)/shard_map/ppermute | solution.py:19
  17.0 24.2 %collective-permute-done.5 = bf16[64,3072]{1,0:T(8,128)(2,1)S(1)} collective-permute-done((bf16[64,3072]{1,0:T(8,128)(2,1)S(1)}, bf16[64,3072]{1,0:T(8,128)(2,1)S(1)}, u32[]{:S(2)}, u32[]{:S(2)}) %collective-permute-start.5) | collective-permute-done | bytes 393248 | tf_op jit(solution)/shard_map/ppermute | solution.py:14
  41.3 3.7 %collective-permute-start.6 = (bf16[64,2816]{1,0:T(8,128)(2,1)S(1)}, bf16[64,2816]{1,0:T(8,128)(2,1)S(1)}, u32[]{:S(2)}, u32[]{:S(2)}) collective-permute-start(bf16[64,2816]{1,0:T(8,128)(2,1)S(1)} %slice.144), channel_id=1, source_target_pairs={{0,4},{4,0},{8,12},{12,8},{16,20},{20,16},{24,28},{28,24},{32,36},... | collective-permute-start | bytes 1081352 | tf_op jit(solution)/shard_map/ppermute | solution.py:19
  45.0 0.1 copy.22
  45.1 0.1 copy.23
  45.2 0.1 iota_compare_fusion
  45.3 0.1 broadcast_in_dim.35
  45.4 0.0 collective-permute-done.1
  45.5 6.9 %collective-permute-done.6 = bf16[64,2816]{1,0:T(8,128)(2,1)S(1)} collective-permute-done((bf16[64,2816]{1,0:T(8,128)(2,1)S(1)}, bf16[64,2816]{1,0:T(8,128)(2,1)S(1)}, u32[]{:S(2)}, u32[]{:S(2)}) %collective-permute-start.6) | collective-permute-done | bytes 360480 | tf_op jit(solution)/shard_map/ppermute | solution.py:19
  52.4 0.0 slice-start
  52.4 0.0 collective-permute-done.2
  52.5 1.8 %fusion.8 = f32[128,512]{1,0:T(8,128)S(1)} fusion(bf16[64,2560]{1,0:T(8,128)(2,1)S(1)} %slice.149, bf16[64,2560]{1,0:T(8,128)(2,1)S(1)} %slice.148, bf16[2560,256]{1,0:T(8,128)(2,1)} %collective-permute-done.2, bf16[2560,256]{1,0:T(8,128)(2,1)S(1)} %bitcast.88), kind=kOutput, calls=%fused_computation.16 | convolution fusion | flops 342097920 | bytes 3538944 | tf_op jit(solution)/shard_map/dot_general | solution.py:27
  54.3 0.1 fusion.47
  54.4 2.3 %fusion.27 = f32[128,2560]{1,0:T(8,128)S(1)} fusion(bf16[128,128]{1,0:T(8,128)(2,1)S(1)} %get-tuple-element.11, bf16[128,128]{1,0:T(8,128)(2,1)S(1)} %get-tuple-element.12, bf16[128,128]{1,0:T(8,128)(2,1)S(1)} %get-tuple-element.13, bf16[128,128]{1,0:T(8,128)(2,1)S(1)} %get-tuple-element.10, bf16[2560,256]{1,0:T(8,128)(2,1)} %collective-permute-done.2, ...), kind=kOutput, calls=%fused_computation.45 | convolution fusion | flops 341311488 | bytes 4063232 | tf_op jit(solution)/shard_map/dot_general | solution.py:39
  56.7 0.0 slice-start.1
  56.7 3.6 %collective-permute-start.7 = (bf16[64,2560]{1,0:T(8,128)(2,1)S(1)}, bf16[64,2560]{1,0:T(8,128)(2,1)S(1)}, u32[]{:S(2)}, u32[]{:S(2)}) collective-permute-start(bf16[64,2560]{1,0:T(8,128)(2,1)S(1)} %slice.206), channel_id=1, source_target_pairs={{0,4},{4,0},{8,12},{12,8},{16,20},{20,16},{24,28},{28,24},{32,36},... | collective-permute-start | bytes 983048 | tf_op jit(solution)/shard_map/ppermute | solution.py:19
  60.4 1.8 %fusion.4 = f32[128,512]{1,0:T(8,128)S(1)} fusion(bf16[64,2560]{1,0:T(8,128)(2,1)S(1)} %slice.133, bf16[64,2560]{1,0:T(8,128)(2,1)S(1)} %bitcast.71, bf16[2560,256]{1,0:T(8,128)(2,1)} %collective-permute-done.2, bf16[2560,256]{1,0:T(8,128)(2,1)S(1)} %bitcast.90), kind=kOutput, calls=%fused_computation.12 | convolution fusion | flops 342097920 | bytes 3538944 | tf_op jit(solution)/shard_map/dot_general | solution.py:27
  62.2 0.1 fusion.37
  62.3 2.3 %fusion.19 = f32[128,2560]{1,0:T(8,128)S(1)} fusion(bf16[128,128]{1,0:T(8,128)(2,1)S(1)} %get-tuple-element.7, bf16[128,128]{1,0:T(8,128)(2,1)S(1)} %get-tuple-element.8, bf16[128,128]{1,0:T(8,128)(2,1)S(1)} %get-tuple-element.9, bf16[128,128]{1,0:T(8,128)(2,1)S(1)} %get-tuple-element.6, bf16[2560,256]{1,0:T(8,128)(2,1)} %collective-permute-done.2, ...), kind=kOutput, calls=%fused_computation.37 | convolution fusion | flops 341311488 | bytes 4063232 | tf_op jit(solution)/shard_map/dot_general | solution.py:39
  64.7 2.2 %collective-permute-start.3 = (bf16[64,2560]{1,0:T(8,128)(2,1)S(1)}, bf16[64,2560]{1,0:T(8,128)(2,1)S(1)}, u32[]{:S(2)}, u32[]{:S(2)}) collective-permute-start(bf16[64,2560]{1,0:T(8,128)(2,1)S(1)} %slice.207), channel_id=1, source_target_pairs={{0,4},{4,0},{8,12},{12,8},{16,20},{20,16},{24,28},{28,24},{32,36},... | collective-permute-start | bytes 983048 | tf_op jit(solution)/shard_map/ppermute | solution.py:19
  66.9 0.6 fusion.2
  67.5 1.9 %collective-permute-start.10 = (bf16[2560,256]{1,0:T(8,128)(2,1)S(1)}, bf16[2560,256]{1,0:T(8,128)(2,1)S(1)}, u32[]{:S(2)}, u32[]{:S(2)}) collective-permute-start(bf16[2560,256]{1,0:T(8,128)(2,1)S(1)} %fusion.2), channel_id=1, source_target_pairs={{0,1},{1,0},{2,3},{3,2},{4,5},{5,4},{6,7},{7,6},{8,9},{9,8},{10,11... | collective-permute-start | bytes 3932168 | tf_op jit(solution)/shard_map/ppermute | solution.py:19
  69.4 0.0 collective-permute-done.7
  69.4 0.1 slice_add_fusion
  69.5 12.0 %collective-permute-start.8 = (bf16[32,2560]{1,0:T(8,128)(2,1)S(1)}, bf16[32,2560]{1,0:T(8,128)(2,1)S(1)}, u32[]{:S(2)}, u32[]{:S(2)}) collective-permute-start(bf16[32,2560]{1,0:T(8,128)(2,1)S(1)} %fusion.15), channel_id=1, source_target_pairs={{0,2},{1,3},{2,0},{3,1},{4,6},{5,7},{6,4},{7,5},{8,10},{9,11},{10,... | collective-permute-start | bytes 491528 | tf_op jit(solution)/shard_map/ppermute | solution.py:19
  81.5 0.0 collective-permute-done.3
  81.5 0.1 slice_add_fusion.1
  81.6 4.4 %collective-permute-start.4 = (bf16[32,2560]{1,0:T(8,128)(2,1)S(1)}, bf16[32,2560]{1,0:T(8,128)(2,1)S(1)}, u32[]{:S(2)}, u32[]{:S(2)}) collective-permute-start(bf16[32,2560]{1,0:T(8,128)(2,1)S(1)} %fusion.14), channel_id=1, source_target_pairs={{0,2},{1,3},{2,0},{3,1},{4,6},{5,7},{6,4},{7,5},{8,10},{9,11},{10,... | collective-permute-start | bytes 491528 | tf_op jit(solution)/shard_map/ppermute | solution.py:19
  86.0 1.7 %collective-permute-done.8 = bf16[32,2560]{1,0:T(8,128)(2,1)S(1)} collective-permute-done((bf16[32,2560]{1,0:T(8,128)(2,1)S(1)}, bf16[32,2560]{1,0:T(8,128)(2,1)S(1)}, u32[]{:S(2)}, u32[]{:S(2)}) %collective-permute-start.8) | collective-permute-done | bytes 163872 | tf_op jit(solution)/shard_map/ppermute | solution.py:19
  87.7 10.2 %collective-permute-start.9 = (bf16[32,2560]{1,0:T(8,128)(2,1)S(1)}, bf16[32,2560]{1,0:T(8,128)(2,1)S(1)}, u32[]{:S(2)}, u32[]{:S(2)}) collective-permute-start(bf16[32,2560]{1,0:T(8,128)(2,1)S(1)} %fusion.12), channel_id=1, source_target_pairs={{0,1016},{4,1020},{8,0},{12,4},{16,8},{20,12},{24,16},{28,20},{32,... | collective-permute-start | bytes 491528 | tf_op jit(solution)/shard_map/ppermute | solution.py:14
  98.0 1.2 %collective-permute-done.4 = bf16[32,2560]{1,0:T(8,128)(2,1)S(1)} collective-permute-done((bf16[32,2560]{1,0:T(8,128)(2,1)S(1)}, bf16[32,2560]{1,0:T(8,128)(2,1)S(1)}, u32[]{:S(2)}, u32[]{:S(2)}) %collective-permute-start.4) | collective-permute-done | bytes 163872 | tf_op jit(solution)/shard_map/ppermute | solution.py:19
  99.2 3.4 %collective-permute-done.9 = bf16[32,2560]{1,0:T(8,128)(2,1)S(1)} collective-permute-done((bf16[32,2560]{1,0:T(8,128)(2,1)S(1)}, bf16[32,2560]{1,0:T(8,128)(2,1)S(1)}, u32[]{:S(2)}, u32[]{:S(2)}) %collective-permute-start.9) | collective-permute-done | bytes 163872 | tf_op jit(solution)/shard_map/ppermute | solution.py:14
  102.6 0.8 bitcast_select_fusion.1
  103.4 0.0 collective-permute-done.10
  103.4 1.6 %fusion.3 = bf16[1,2560,256]{2,1,0:T(8,128)(2,1)} fusion(bf16[2560,256]{1,0:T(8,128)(2,1)S(1)} %collective-permute-done.10, bf16[64,2560]{1,0:T(8,128)(2,1)S(1)} %slice.149, bf16[64,2560]{1,0:T(8,128)(2,1)S(1)} %slice.148, bf16[64,2560]{1,0:T(8,128)(2,1)S(1)} %slice.133, bf16[64,2560]{1,0:T(8,128)(2,1)S(1)} %bitcast.73, ...), kind=kOutput, calls=%fused_computation.5 | convolution fusion | flops 343408640 | bytes 4063232 | tf_op jit(solution)/shard_map/dot_general | solution.py:43
  (37 shorter events, 0.6 us)
Async XLA Ops:
  0.6 7.2 %copy-start = (bf16[256,2560]{1,0:T(8,128)(2,1)S(1)}, bf16[256,2560]{1,0:T(8,128)(2,1)}, u32[]{:S(2)}) copy-start(bf16[256,2560]{1,0:T(8,128)(2,1)} %param.5) | copy-start | bytes 3932164
  1.7 6.4 %collective-permute-start = (bf16[2,2,32,256]{3,2,1,0:T(8,128)(2,1)S(1)}, bf16[2,2,32,256]{3,2,1,0:T(8,128)(2,1)S(1)}, u32[]{:S(2)}, u32[]{:S(2)}) collective-permute-start(bf16[2,2,32,256]{3,2,1,0:T(8,128)(2,1)S(1)} %get-tuple-element.15), channel_id=1, source_target_pairs={{0,1},{1,0},{2,3},{3,2},{4,5},{5,4},{6,7},{7,6},{8,9},{9,8},{10,11... | collective-permute-start | bytes 196616 | tf_op jit(solution)/shard_map/ppermute | solution.py:19
  3.6 48.8 %collective-permute-start.2 = (bf16[2560,256]{1,0:T(8,128)(2,1)}, bf16[2560,256]{1,0:T(8,128)(2,1)}, u32[]{:S(2)}, u32[]{:S(2)}) collective-permute-start(bf16[2560,256]{1,0:T(8,128)(2,1)} %bitcast.87), channel_id=1, source_target_pairs={{0,1},{1,0},{2,3},{3,2},{4,5},{5,4},{6,7},{7,6},{8,9},{9,8},{10,11... | collective-permute-start | bytes 3932168 | tf_op jit(solution)/shard_map/ppermute | solution.py:19
  8.7 32.6 %collective-permute-start.5 = (bf16[64,3072]{1,0:T(8,128)(2,1)S(1)}, bf16[64,3072]{1,0:T(8,128)(2,1)S(1)}, u32[]{:S(2)}, u32[]{:S(2)}) collective-permute-start(bf16[64,3072]{1,0:T(8,128)(2,1)S(1)} %pad_maximum_fusion.2), channel_id=1, source_target_pairs={{0,8},{4,12},{8,16},{12,20},{16,24},{20,28},{24,32},{28,36},{32,40... | collective-permute-start | bytes 1179656 | tf_op jit(solution)/shard_map/ppermute | solution.py:14
  13.4 32.0 %collective-permute-start.1 = (bf16[64,2816]{1,0:T(8,128)(2,1)S(1)}, bf16[64,2816]{1,0:T(8,128)(2,1)S(1)}, u32[]{:S(2)}, u32[]{:S(2)}) collective-permute-start(bf16[64,2816]{1,0:T(8,128)(2,1)S(1)} %pad_maximum_fusion.3), channel_id=1, source_target_pairs={{0,4},{4,0},{8,12},{12,8},{16,20},{20,16},{24,28},{28,24},{32,36},... | collective-permute-start | bytes 1081352 | tf_op jit(solution)/shard_map/ppermute | solution.py:19
  41.3 11.1 %copy-start.1 = (bf16[64,3072]{1,0:T(8,128)(2,1)}, bf16[64,3072]{1,0:T(8,128)(2,1)S(1)}, u32[]{:S(2)}) copy-start(bf16[64,3072]{1,0:T(8,128)(2,1)S(1)} %collective-permute-done.5) | copy-start | bytes 1179652
  41.3 11.1 %collective-permute-start.6 = (bf16[64,2816]{1,0:T(8,128)(2,1)S(1)}, bf16[64,2816]{1,0:T(8,128)(2,1)S(1)}, u32[]{:S(2)}, u32[]{:S(2)}) collective-permute-start(bf16[64,2816]{1,0:T(8,128)(2,1)S(1)} %slice.144), channel_id=1, source_target_pairs={{0,4},{4,0},{8,12},{12,8},{16,20},{20,16},{24,28},{28,24},{32,36},... | collective-permute-start | bytes 1081352 | tf_op jit(solution)/shard_map/ppermute | solution.py:19
  45.4 7.0 %copy-start.3 = (bf16[1,2560,256]{2,1,0:T(8,128)(2,1)S(1)}, bf16[1,2560,256]{2,1,0:T(8,128)(2,1)}, u32[]{:S(2)}) copy-start(bf16[1,2560,256]{2,1,0:T(8,128)(2,1)} %param.9) | copy-start | bytes 3932164
  45.4 8.9 %copy-start.2 = (bf16[64,2816]{1,0:T(8,128)(2,1)}, bf16[64,2816]{1,0:T(8,128)(2,1)S(1)}, u32[]{:S(2)}) copy-start(bf16[64,2816]{1,0:T(8,128)(2,1)S(1)} %collective-permute-done.1) | copy-start | bytes 1081348
  52.4 1.9 %slice-start = ((bf16[64,3072]{1,0:T(8,128)(2,1)}), bf16[64,256]{1,0:T(8,128)(2,1)S(1)}, s32[]{:S(2)}) async-start(bf16[64,3072]{1,0:T(8,128)(2,1)} %copy-done.1), calls=%async_computation | async-start | bytes 65536 | tf_op jit(solution)/shard_map/slice | solution.py:93
  56.7 5.5 %slice-start.1 = ((bf16[64,2816]{1,0:T(8,128)(2,1)}), bf16[64,256]{1,0:T(8,128)(2,1)S(1)}, s32[]{:S(2)}) async-start(bf16[64,2816]{1,0:T(8,128)(2,1)} %copy-done.2), calls=%async_computation.1 | async-start | bytes 65536 | tf_op jit(solution)/shard_map/slice | solution.py:91
  56.7 12.7 %collective-permute-start.7 = (bf16[64,2560]{1,0:T(8,128)(2,1)S(1)}, bf16[64,2560]{1,0:T(8,128)(2,1)S(1)}, u32[]{:S(2)}, u32[]{:S(2)}) collective-permute-start(bf16[64,2560]{1,0:T(8,128)(2,1)S(1)} %slice.206), channel_id=1, source_target_pairs={{0,4},{4,0},{8,12},{12,8},{16,20},{20,16},{24,28},{28,24},{32,36},... | collective-permute-start | bytes 983048 | tf_op jit(solution)/shard_map/ppermute | solution.py:19
  64.7 16.8 %collective-permute-start.3 = (bf16[64,2560]{1,0:T(8,128)(2,1)S(1)}, bf16[64,2560]{1,0:T(8,128)(2,1)S(1)}, u32[]{:S(2)}, u32[]{:S(2)}) collective-permute-start(bf16[64,2560]{1,0:T(8,128)(2,1)S(1)} %slice.207), channel_id=1, source_target_pairs={{0,4},{4,0},{8,12},{12,8},{16,20},{20,16},{24,28},{28,24},{32,36},... | collective-permute-start | bytes 983048 | tf_op jit(solution)/shard_map/ppermute | solution.py:19
  67.5 36.0 %collective-permute-start.10 = (bf16[2560,256]{1,0:T(8,128)(2,1)S(1)}, bf16[2560,256]{1,0:T(8,128)(2,1)S(1)}, u32[]{:S(2)}, u32[]{:S(2)}) collective-permute-start(bf16[2560,256]{1,0:T(8,128)(2,1)S(1)} %fusion.2), channel_id=1, source_target_pairs={{0,1},{1,0},{2,3},{3,2},{4,5},{5,4},{6,7},{7,6},{8,9},{9,8},{10,11... | collective-permute-start | bytes 3932168 | tf_op jit(solution)/shard_map/ppermute | solution.py:19
  69.5 18.2 %collective-permute-start.8 = (bf16[32,2560]{1,0:T(8,128)(2,1)S(1)}, bf16[32,2560]{1,0:T(8,128)(2,1)S(1)}, u32[]{:S(2)}, u32[]{:S(2)}) collective-permute-start(bf16[32,2560]{1,0:T(8,128)(2,1)S(1)} %fusion.15), channel_id=1, source_target_pairs={{0,2},{1,3},{2,0},{3,1},{4,6},{5,7},{6,4},{7,5},{8,10},{9,11},{10,... | collective-permute-start | bytes 491528 | tf_op jit(solution)/shard_map/ppermute | solution.py:19
  81.6 17.5 %collective-permute-start.4 = (bf16[32,2560]{1,0:T(8,128)(2,1)S(1)}, bf16[32,2560]{1,0:T(8,128)(2,1)S(1)}, u32[]{:S(2)}, u32[]{:S(2)}) collective-permute-start(bf16[32,2560]{1,0:T(8,128)(2,1)S(1)} %fusion.14), channel_id=1, source_target_pairs={{0,2},{1,3},{2,0},{3,1},{4,6},{5,7},{6,4},{7,5},{8,10},{9,11},{10,... | collective-permute-start | bytes 491528 | tf_op jit(solution)/shard_map/ppermute | solution.py:19
  87.7 14.8 %collective-permute-start.9 = (bf16[32,2560]{1,0:T(8,128)(2,1)S(1)}, bf16[32,2560]{1,0:T(8,128)(2,1)S(1)}, u32[]{:S(2)}, u32[]{:S(2)}) collective-permute-start(bf16[32,2560]{1,0:T(8,128)(2,1)S(1)} %fusion.12), channel_id=1, source_target_pairs={{0,1016},{4,1020},{8,0},{12,4},{16,8},{20,12},{24,16},{28,20},{32,... | collective-permute-start | bytes 491528 | tf_op jit(solution)/shard_map/ppermute | solution.py:14

commit v2 on v1

v2 whole, which is shorter than its diff:
```python
import math

import jax
import jax.numpy as jnp
from jax import lax
from jax.experimental import pallas as pl
from jax.experimental.pallas import tpu as pltpu
from jax.sharding import PartitionSpec as P

BF = jnp.bfloat16
F32 = jnp.float32


def moved(value, node_step, node_flip, local_flip):
    nodes, in_node = lax.axis_size("node"), lax.axis_size("local")
    route = []
    for n in range(nodes):
        for l in range(in_node):
            target = ((n + node_step) % nodes) ^ node_flip
            route.append((n * in_node + l, target * in_node + (l ^ local_flip)))
    return lax.ppermute(value, ("node", "local"), route)


def pick(array, index, axis):
    return lax.dynamic_index_in_dim(array, index, axis, keepdims=False)


def expert_kernel(own_ref, own_cot_ref, got_ref, got_cot_ref, own_w_ref, other_w_ref, dh_ref, give_ref, keep_ref):
    half, dim = keep_ref.shape
    width = own_w_ref.shape[1] // 2
    x = jnp.concatenate([own_ref[:, :dim], got_ref[:, :dim]], axis=0)
    cot = jnp.concatenate([own_cot_ref[...], got_cot_ref[...]], axis=0)
    weights = (own_w_ref, other_w_ref)
    dhs = []
    for k in range(2):
        hidden = jnp.dot(x, weights[k][...], preferred_element_type=F32)
        gate = hidden[:, :width]
        up = hidden[:, width:]
        c = cot[:, k * width : (k + 1) * width].astype(F32)
        s = jax.nn.sigmoid(gate)
        cs = c * s
        dh = jnp.concatenate([cs * up * (1.0 + gate * (1.0 - s)), cs * gate], axis=1).astype(BF)
        dh_ref[:, 2 * k * width : 2 * (k + 1) * width] = dh
        dhs.append(dh)
    step = 512
    for first in range(0, dim, step):
        total = None
        for k in range(2):
            part = lax.dot_general(
                dhs[k],
                weights[k][first : first + step, :],
                (((1,), (1,)), ((), ())),
                preferred_element_type=F32,
            )
            total = part if total is None else total + part
        keep_ref[:, first : first + step] = total[:half]
        give_ref[:, first : first + step] = total[half:].astype(BF)


def expert_work(own, own_cot, got, got_cot, own_w, other_w):
    half = own.shape[0]
    dim, wide = own_w.shape
    vmem = pl.BlockSpec(memory_space=pltpu.VMEM)
    return pl.pallas_call(
        expert_kernel,
        out_shape=(
            jax.ShapeDtypeStruct((2 * half, 2 * wide), BF),
            jax.ShapeDtypeStruct((half, dim), BF),
            jax.ShapeDtypeStruct((half, dim), F32),
        ),
        in_specs=[vmem] * 6,
        out_specs=(vmem,) * 3,
        compiler_params=pltpu.CompilerParams(vmem_limit_bytes=32 * 1024 * 1024),
        cost_estimate=pl.CostEstimate(
            flops=8 * half * dim * wide * 2, bytes_accessed=8 * 1024 * 1024, transcendentals=2 * half * wide
        ),
    )(own, own_cot, got, got_cot, own_w, other_w)


def weight_grads(rows, dh):
    return lax.dot_general(rows, dh, (((0,), (0,)), ((), ())), preferred_element_type=F32)


def on_device(x_groups, group_len, act_grad, slot_gate, gate_up):
    node_rows, dim = x_groups.shape
    in_node = lax.axis_size("local")
    far_count = in_node // 2
    cap = node_rows // (2 * in_node)
    width = gate_up.shape[2] // 2
    half = far_count * cap
    node = lax.axis_index("node")
    local = lax.axis_index("local")
    core = local % 2
    far = local // 2
    parity = node % 2
    factor = 1.0 / math.sqrt(4 * in_node * cap)

    own_w = gate_up[0]

    def rows_of(array, k):
        shaped = array.reshape(far_count, 2, 2, cap, dim)
        return lax.dynamic_slice(
            shaped, (0, core, k, 0, 0), (far_count, 1, 1, cap, dim)
        ).reshape(half, dim)

    rows1 = rows_of(x_groups, 1)
    rows1, act_grad, x_groups, own_w = lax.optimization_barrier((rows1, act_grad, x_groups, own_w))
    own1 = moved(rows1, 2, 0, 0)

    acts = act_grad.reshape(far_count, 2, 2, cap, 2 * width)
    act_other = moved(pick(acts, 1 - core, 1), 0, 0, 1)
    act_mine = pick(acts, core, 1)
    lengths = pick(group_len, node, 0)
    alive = jnp.arange(cap)[None, None, :] < lengths[:, :, None]
    gates = jnp.where(alive.reshape(node_rows), slot_gate, jnp.zeros_like(slot_gate))
    gates = pick(gates.reshape(far_count, 2, 2, cap), core, 1).astype(F32)

    def cots(which):
        cut_to = [
            pick(a.reshape(far_count, 2, cap, 2, width), which, 3) for a in (act_mine, act_other)
        ]
        both = jnp.concatenate(cut_to, axis=-1).astype(F32)
        return (both * gates[..., None]).astype(BF)

    def group(array, k):
        return array[:, k].reshape(half, array.shape[-1])

    keep = cots(parity)
    give = cots(1 - parity)
    own0 = jnp.concatenate([rows_of(x_groups, 0), group(give, 0)], axis=1)
    got0 = moved(own0, 0, 1, 0)
    other_w = moved(own_w, 0, 0, 1)
    cots1 = moved(jnp.concatenate([group(give, 1), group(keep, 1)], axis=1), 2, 0, 0)

    got1 = moved(jnp.concatenate([own1, cots1[:, : 2 * width]], axis=1), 0, 1, 0)
    dh0, send0, kept0 = expert_work(own0, group(keep, 0), got0, got0[:, dim:], own_w, other_w)
    got1, _ = lax.optimization_barrier((got1, kept0))
    back0 = moved(send0, 0, 1, 0)
    dh1, send1, kept1 = expert_work(own1, cots1[:, 2 * width :], got1, got1[:, dim:], own_w, other_w)
    back1 = moved(send1, 0, 1, 0)

    all_rows = [own0[:, :dim], got0[:, :dim], own1, got1[:, :dim]]
    all_rows = jnp.concatenate(all_rows, axis=0)
    all_dh = jnp.concatenate([dh0, dh1], axis=0)
    other_dw = (weight_grads(all_rows, all_dh[:, 2 * width :]) * factor).astype(BF)
    other_dw = moved(other_dw, 0, 0, 1)

    sum1 = (kept1 + back1.astype(F32)).reshape(far_count, cap, dim)
    _, back0 = lax.optimization_barrier((sum1, back0))
    away1 = moved(pick(sum1, 1 - far, 0).astype(BF), 0, 0, 2)
    sum0 = (kept0 + back0.astype(F32)).reshape(far_count, cap, dim)
    away0 = moved(pick(sum0, 1 - far, 0).astype(BF), 0, 0, 2)
    out1 = (pick(sum1, far, 0) + away1.astype(F32)).astype(BF)
    out1 = moved(out1, -2, 0, 0)
    out0 = pick(sum0, far, 0) + away0.astype(F32)

    own_dw = weight_grads(all_rows, all_dh[:, : 2 * width]) * factor
    grad_weights = (own_dw + other_dw.astype(F32)).astype(BF)
    out1, grad_weights = lax.optimization_barrier((out1, grad_weights))

    mine = pick(alive, local, 0)
    finished = jnp.stack([out0, out1.astype(F32)], axis=0)
    finished = jnp.where(mine[:, :, None], finished, jnp.zeros_like(finished)).astype(BF)
    return (finished.reshape(2 * cap, dim), grad_weights[None])


def solution(mesh):
    placed = (P("node", None), P(), P("node", "local"), P("node"), P("node", None, "local"))
    return jax.shard_map(
        on_device,
        mesh=mesh,
        in_specs=placed,
        out_specs=(P(("node", "local"), None), P("node", None, "local")),
        check_vma=False,
    )
```

time: 107 us -> 99.7 us (0.932); the launches traced: 105 us -> 99 us
  waiting for transfers between devices: 37.4 us -> 25.9 us
  matrix products: 10.4 us -> 2.18 us
  Pallas kernels: 0 us -> 5.66 us
  local copies, waits for them, and re-layouts: 3.64 us -> 7.94 us
  starting transfers between devices: 50.7 us -> 53.6 us
    ppermute x11 -> x12, waiting for transfers between devices: 37.4 us -> 25.9 us  [moved(): return lax.ppermute(value, ('node', 'local'), route)]
    dot_general x4 -> x0, matrix products: 8.22 us -> none  [the longest x2 4.57 us: row_grads(): lax.dot_general(dh, weights, (((1,), (1,)), ((), ())), preferred_element_...]
    pallas_call x0 -> x2, Pallas kernels: none -> 5.66 us  [expert_work(): pl.pallas_call(expert_kernel, out_shape=(jax.ShapeDtypeStruct((2 * half,...]
    ppermute x11 -> x12, starting transfers between devices: 50.7 us -> 53.6 us  [moved(): return lax.ppermute(value, ('node', 'local'), route)]
    unnamed x13 -> x18, local copies, waits for them, and re-layouts: 1.04 us -> 2.96 us
    slice x11 -> x5, local copies, waits for them, and re-layouts: 0.18 us -> 1.79 us  [the longest x2 1.02 us: on_device(): all_rows = [own0[:, :dim], got0[:, :dim], own1, got1[:, :dim]]]
    dynamic_slice x0 -> x2, local copies, waits for them, and re-layouts: none -> 1.54 us  [rows_of(): lax.dynamic_slice(shaped, (0, core, k, 0, 0), (far_count, 1, 1, cap, dim))]
  transfers between devices with their start and end apart: 11 -> 12, of which waited for: 5 -> 5; matrix products, arithmetic and copies ran while one was open for 8% -> 8% of each run, Pallas kernels for 0% -> 3%
where the time goes in v2:
time: 99.7 us; the launch traced here: 99 us
  starting transfers between devices  53.6 us (54%)
  waiting for transfers between devices  25.9 us (26%)
  local copies, waits for them, and re-layouts  7.94 us (8%)
  Pallas kernels  5.66 us (6%)
  other arithmetic  2.69 us (3%)
  matrix products  2.18 us (2%)
  between operations  1.08 us (1%)
    ppermute x12, starting transfers between devices, moved(): return lax.ppermute(value, ('node', 'local'), route)  53.6 us
    ppermute x12, waiting for transfers between devices, moved(): return lax.ppermute(value, ('node', 'local'), route)  25.9 us
    pallas_call x2, Pallas kernels, expert_work(): pl.pallas_call(expert_kernel, out_shape=(jax.ShapeDtypeStruct((2 * half,...  5.66 us
    unnamed x18, local copies, waits for them, and re-layouts  2.96 us
    dot_general x2, matrix products, weight_grads(): lax.dot_general(rows, dh, (((0,), (0,)), ((), ())), preferred_element_typ...  2.18 us
  transfers between devices with their start and end apart: 12, of which 5 were waited for; matrix products, arithmetic and copies ran while one was open for 8% of the time, Pallas kernels for 3%

profile of v2, /device:TPU:14, one launch (start us, length us, event | category | flops | bytes accessed | tf_op | source)
XLA Modules:
  0.0 99.0 jit_solution(12791170158867160530)
XLA Ops:
  0.6 0.0 copy-start
  0.7 1.3 %copy-done = bf16[256,2560]{1,0:T(8,128)(2,1)S(1)} copy-done((bf16[256,2560]{1,0:T(8,128)(2,1)S(1)}, bf16[256,2560]{1,0:T(8,128)(2,1)}, u32[]{:S(2)}) %copy-start) | copy-done | bytes 1310744
  2.0 0.7 constant_dynamic-slice_fusion.6
  2.7 0.9 dynamic-slice_bitcast_fusion.1
  3.6 1.9 %collective-permute-start = (bf16[2,2,32,256]{3,2,1,0:T(8,128)(2,1)S(1)}, bf16[2,2,32,256]{3,2,1,0:T(8,128)(2,1)S(1)}, u32[]{:S(2)}, u32[]{:S(2)}) collective-permute-start(bf16[2,2,32,256]{3,2,1,0:T(8,128)(2,1)S(1)} %get-tuple-element.31), channel_id=1, source_target_pairs={{0,1},{1,0},{2,3},{3,2},{4,5},{5,4},{6,7},{7,6},{8,9},{9,8},{10,11... | collective-permute-start | bytes 196616 | tf_op jit(solution)/shard_map/ppermute | solution.py:21
  5.5 4.7 %collective-permute-start.3 = (bf16[64,2560]{1,0:T(8,128)(2,1)}, bf16[64,2560]{1,0:T(8,128)(2,1)S(1)}, u32[]{:S(2)}, u32[]{:S(2)}) collective-permute-start(bf16[64,2560]{1,0:T(8,128)(2,1)} %bitcast.2), channel_id=1, source_target_pairs={{0,8},{1,9},{2,10},{3,11},{4,12},{5,13},{6,14},{7,15},{8,16},{9,17... | collective-permute-start | bytes 983048 | tf_op jit(solution)/shard_map/ppermute | solution.py:21
  10.2 2.1 %collective-permute-start.2 = (bf16[2560,256]{1,0:T(8,128)(2,1)}, bf16[2560,256]{1,0:T(8,128)(2,1)}, u32[]{:S(2)}, u32[]{:S(2)}) collective-permute-start(bf16[2560,256]{1,0:T(8,128)(2,1)} %bitcast.69), channel_id=1, source_target_pairs={{0,1},{1,0},{2,3},{3,2},{4,5},{5,4},{6,7},{7,6},{8,9},{9,8},{10,11... | collective-permute-start | bytes 3932168 | tf_op jit(solution)/shard_map/ppermute | solution.py:21
  12.4 0.8 constant_dynamic-slice_fusion.8
  13.2 0.1 copy.18
  13.3 0.1 copy.19
  13.4 0.1 iota_compare_fusion
  13.4 0.1 lt.77
  13.5 0.7 broadcast_select_fusion
  14.2 0.1 reshape.65
  14.3 0.8 constant_dynamic-slice_fusion.5
  15.1 0.0 collective-permute-done
  15.1 0.3 constant_dynamic-slice_fusion.3
  15.5 0.1 multiply_convert_fusion.1
  15.6 0.0 copy-start.1
  15.7 6.1 %collective-permute-start.4 = (bf16[64,512]{1,0:T(8,128)(2,1)S(1)}, bf16[64,512]{1,0:T(8,128)(2,1)S(1)}, u32[]{:S(2)}, u32[]{:S(2)}) collective-permute-start(bf16[64,512]{1,0:T(8,128)(2,1)S(1)} %pad_maximum_fusion.6), channel_id=1, source_target_pairs={{0,8},{1,9},{2,10},{3,11},{4,12},{5,13},{6,14},{7,15},{8,16},{9,17... | collective-permute-start | bytes 196616 | tf_op jit(solution)/shard_map/ppermute | solution.py:21
  21.8 2.7 %collective-permute-start.1 = (bf16[64,2816]{1,0:T(8,128)(2,1)S(1)}, bf16[64,2816]{1,0:T(8,128)(2,1)}, u32[]{:S(2)}, u32[]{:S(2)}) collective-permute-start(bf16[64,2816]{1,0:T(8,128)(2,1)S(1)} %pad_maximum_fusion.2.own_ref), channel_id=1, source_target_pairs={{0,4},{1,5},{2,6},{3,7},{4,0},{5,1},{6,2},{7,3},{8,12},{9,13},{10,... | collective-permute-start | bytes 1081352 | tf_op jit(solution)/shard_map/ppermute | solution.py:21
  24.5 14.2 %collective-permute-done.4 = bf16[64,512]{1,0:T(8,128)(2,1)S(1)} collective-permute-done((bf16[64,512]{1,0:T(8,128)(2,1)S(1)}, bf16[64,512]{1,0:T(8,128)(2,1)S(1)}, u32[]{:S(2)}, u32[]{:S(2)}) %collective-permute-start.4) | collective-permute-done | bytes 65568 | tf_op jit(solution)/shard_map/ppermute | solution.py:21
  38.7 0.0 collective-permute-done.3.own_ref
  38.7 0.8 pad_maximum_fusion.3
  39.5 0.7 copy-done.2
  40.2 3.8 %collective-permute-start.5 = (bf16[64,2816]{1,0:T(8,128)(2,1)}, bf16[64,2816]{1,0:T(8,128)(2,1)S(1)}, u32[]{:S(2)}, u32[]{:S(2)}) collective-permute-start(bf16[64,2816]{1,0:T(8,128)(2,1)} %pad_maximum_fusion.3), channel_id=1, source_target_pairs={{0,4},{1,5},{2,6},{3,7},{4,0},{5,1},{6,2},{7,3},{8,12},{9,13},{10,... | collective-permute-start | bytes 1081352 | tf_op jit(solution)/shard_map/ppermute | solution.py:21
  44.1 0.1 broadcast_in_dim.24
  44.1 0.0 collective-permute-done.1.got_ref
  44.1 0.8 slice.50.got_cot_ref
  44.9 1.0 %slice.55 = bf16[64,2560]{1,0:T(8,128)(2,1)S(1)} slice(bf16[64,2816]{1,0:T(8,128)(2,1)} %collective-permute-done.1.got_ref), slice={[0:64], [0:2560]} | slice | bytes 655360 | tf_op jit(solution)/shard_map/slice | solution.py:142
  45.9 0.0 copy-start.3
  45.9 2.9 %shard_map.68 = (bf16[128,512]{1,0:T(8,128)(2,1)S(1)}, bf16[64,2560]{1,0:T(8,128)(2,1)S(1)}, f32[64,2560]{1,0:T(8,128)S(1)}) custom-call(bf16[64,2816]{1,0:T(8,128)(2,1)S(1)} %pad_maximum_fusion.2.own_ref, bf16[64,256]{1,0:T(8,128)(2,1)S(1)} %bitcast.72, bf16[64,2816]{1,0:T(8,128)(2,1)} %collective-permute-done.1.got_ref, ...), custom_call_target="tpu_custom_call" | custom-call | flops 671088640 | bytes 8388608 | tf_op jit(solution)/shard_map/pallas_call | solution.py:64
  48.8 3.6 %collective-permute-done.5.got_ref = bf16[64,2816]{1,0:T(8,128)(2,1)S(1)} collective-permute-done((bf16[64,2816]{1,0:T(8,128)(2,1)}, bf16[64,2816]{1,0:T(8,128)(2,1)S(1)}, u32[]{:S(2)}, u32[]{:S(2)}) %collective-permute-start.5) | collective-permute-done | bytes 360480 | tf_op jit(solution)/shard_map/ppermute | solution.py:21
  52.5 2.8 %shard_map.69 = (bf16[128,512]{1,0:T(8,128)(2,1)S(1)}, bf16[64,2560]{1,0:T(8,128)(2,1)S(1)}, f32[64,2560]{1,0:T(8,128)S(1)}) custom-call(bf16[64,2560]{1,0:T(8,128)(2,1)S(1)} %copy-done.3, bf16[64,256]{1,0:T(8,128)(2,1)S(1)} %get-tuple-element.37.own_cot_ref, bf16[64,2816]{1,0:T(8,128)(2,1)S(1)} %collective-permute-done.5.got_ref, ...), custom_call_target="tpu_custom_call" | custom-call | flops 671088640 | bytes 8388608 | tf_op jit(solution)/shard_map/pallas_call | solution.py:64
  55.3 3.6 %collective-permute-start.6 = (bf16[64,2560]{1,0:T(8,128)(2,1)S(1)}, bf16[64,2560]{1,0:T(8,128)(2,1)S(1)}, u32[]{:S(2)}, u32[]{:S(2)}) collective-permute-start(bf16[64,2560]{1,0:T(8,128)(2,1)S(1)} %get-tuple-element.23), channel_id=1, source_target_pairs={{0,4},{1,5},{2,6},{3,7},{4,0},{5,1},{6,2},{7,3},{8,12},{9,13},{10,... | collective-permute-start | bytes 983048 | tf_op jit(solution)/shard_map/ppermute | solution.py:21
  58.9 2.2 %collective-permute-start.7 = (bf16[64,2560]{1,0:T(8,128)(2,1)S(1)}, bf16[64,2560]{1,0:T(8,128)(2,1)S(1)}, u32[]{:S(2)}, u32[]{:S(2)}) collective-permute-start(bf16[64,2560]{1,0:T(8,128)(2,1)S(1)} %get-tuple-element.24), channel_id=1, source_target_pairs={{0,4},{1,5},{2,6},{3,7},{4,0},{5,1},{6,2},{7,3},{8,12},{9,13},{10,... | collective-permute-start | bytes 983048 | tf_op jit(solution)/shard_map/ppermute | solution.py:21
  61.1 0.6 fusion.2
  61.7 1.9 %collective-permute-start.11 = (bf16[2560,256]{1,0:T(8,128)(2,1)S(1)}, bf16[2560,256]{1,0:T(8,128)(2,1)S(1)}, u32[]{:S(2)}, u32[]{:S(2)}) collective-permute-start(bf16[2560,256]{1,0:T(8,128)(2,1)S(1)} %fusion.2), channel_id=1, source_target_pairs={{0,1},{1,0},{2,3},{3,2},{4,5},{5,4},{6,7},{7,6},{8,9},{9,8},{10,11... | collective-permute-start | bytes 3932168 | tf_op jit(solution)/shard_map/ppermute | solution.py:21
  63.6 4.2 %collective-permute-done.6 = bf16[64,2560]{1,0:T(8,128)(2,1)S(1)} collective-permute-done((bf16[64,2560]{1,0:T(8,128)(2,1)S(1)}, bf16[64,2560]{1,0:T(8,128)(2,1)S(1)}, u32[]{:S(2)}, u32[]{:S(2)}) %collective-permute-start.6) | collective-permute-done | bytes 327712 | tf_op jit(solution)/shard_map/ppermute | solution.py:21
  67.8 0.1 convert_add_fusion.1
  67.9 11.8 %collective-permute-start.9 = (bf16[32,2560]{1,0:T(8,128)(2,1)S(1)}, bf16[32,2560]{1,0:T(8,128)(2,1)S(1)}, u32[]{:S(2)}, u32[]{:S(2)}) collective-permute-start(bf16[32,2560]{1,0:T(8,128)(2,1)S(1)} %fusion.7), channel_id=1, source_target_pairs={{0,2},{1,3},{2,0},{3,1},{4,6},{5,7},{6,4},{7,5},{8,10},{9,11},{10,... | collective-permute-start | bytes 491528 | tf_op jit(solution)/shard_map/ppermute | solution.py:21
  79.8 0.1 convert_add_fusion
  79.9 4.6 %collective-permute-start.8 = (bf16[32,2560]{1,0:T(8,128)(2,1)S(1)}, bf16[32,2560]{1,0:T(8,128)(2,1)S(1)}, u32[]{:S(2)}, u32[]{:S(2)}) collective-permute-start(bf16[32,2560]{1,0:T(8,128)(2,1)S(1)} %fusion.6), channel_id=1, source_target_pairs={{0,2},{1,3},{2,0},{3,1},{4,6},{5,7},{6,4},{7,5},{8,10},{9,11},{10,... | collective-permute-start | bytes 491528 | tf_op jit(solution)/shard_map/ppermute | solution.py:21
  84.6 8.0 %collective-permute-start.10 = (bf16[32,2560]{1,0:T(8,128)(2,1)S(1)}, bf16[32,2560]{1,0:T(8,128)(2,1)S(1)}, u32[]{:S(2)}, u32[]{:S(2)}) collective-permute-start(bf16[32,2560]{1,0:T(8,128)(2,1)S(1)} %fusion.4), channel_id=1, source_target_pairs={{0,1016},{1,1017},{2,1018},{3,1019},{4,1020},{5,1021},{6,1022},{7,... | collective-permute-start | bytes 491528 | tf_op jit(solution)/shard_map/ppermute | solution.py:21
  92.5 0.1 collective-permute-done.8
  92.7 1.6 %fusion.1 = bf16[2560,256]{1,0:T(8,128)(2,1)} fusion(bf16[2560,256]{1,0:T(8,128)(2,1)S(1)} %collective-permute-done.11, bf16[64,2560]{1,0:T(8,128)(2,1)S(1)} %slice.45, bf16[64,2560]{1,0:T(8,128)(2,1)S(1)} %copy-done.3, bf16[64,2560]{1,0:T(8,128)(2,1)S(1)} %slice.55, bf16[64,2560]{1,0:T(8,128)(2,1)S(1)} %bitcast.79, ...), kind=kOutput, calls=%fused_computation.3 | convolution fusion | flops 343408640 | bytes 4063232 | tf_op jit(solution)/shard_map/dot_general | solution.py:81
  94.3 3.8 %collective-permute-done.10 = bf16[32,2560]{1,0:T(8,128)(2,1)S(1)} collective-permute-done((bf16[32,2560]{1,0:T(8,128)(2,1)S(1)}, bf16[32,2560]{1,0:T(8,128)(2,1)S(1)}, u32[]{:S(2)}, u32[]{:S(2)}) %collective-permute-start.10) | collective-permute-done | bytes 163872 | tf_op jit(solution)/shard_map/ppermute | solution.py:21
  98.2 0.9 fusion.3
  (33 shorter events, 0.4 us)
Async XLA Ops:
  0.6 1.3 %copy-start = (bf16[256,2560]{1,0:T(8,128)(2,1)S(1)}, bf16[256,2560]{1,0:T(8,128)(2,1)}, u32[]{:S(2)}) copy-start(bf16[256,2560]{1,0:T(8,128)(2,1)} %param.5) | copy-start | bytes 3932164
  3.6 11.5 %collective-permute-start = (bf16[2,2,32,256]{3,2,1,0:T(8,128)(2,1)S(1)}, bf16[2,2,32,256]{3,2,1,0:T(8,128)(2,1)S(1)}, u32[]{:S(2)}, u32[]{:S(2)}) collective-permute-start(bf16[2,2,32,256]{3,2,1,0:T(8,128)(2,1)S(1)} %get-tuple-element.31), channel_id=1, source_target_pairs={{0,1},{1,0},{2,3},{3,2},{4,5},{5,4},{6,7},{7,6},{8,9},{9,8},{10,11... | collective-permute-start | bytes 196616 | tf_op jit(solution)/shard_map/ppermute | solution.py:21
  5.5 33.2 %collective-permute-start.3 = (bf16[64,2560]{1,0:T(8,128)(2,1)}, bf16[64,2560]{1,0:T(8,128)(2,1)S(1)}, u32[]{:S(2)}, u32[]{:S(2)}) collective-permute-start(bf16[64,2560]{1,0:T(8,128)(2,1)} %bitcast.2), channel_id=1, source_target_pairs={{0,8},{1,9},{2,10},{3,11},{4,12},{5,13},{6,14},{7,15},{8,16},{9,17... | collective-permute-start | bytes 983048 | tf_op jit(solution)/shard_map/ppermute | solution.py:21
  10.2 35.7 %collective-permute-start.2 = (bf16[2560,256]{1,0:T(8,128)(2,1)}, bf16[2560,256]{1,0:T(8,128)(2,1)}, u32[]{:S(2)}, u32[]{:S(2)}) collective-permute-start(bf16[2560,256]{1,0:T(8,128)(2,1)} %bitcast.69), channel_id=1, source_target_pairs={{0,1},{1,0},{2,3},{3,2},{4,5},{5,4},{6,7},{7,6},{8,9},{9,8},{10,11... | collective-permute-start | bytes 3932168 | tf_op jit(solution)/shard_map/ppermute | solution.py:21
  15.1 6.6 %copy-start.4 = (bf16[2,1,1,32,2560]{4,3,2,1,0:T(8,128)(2,1)S(1)}, bf16[2,1,1,32,2560]{4,3,2,1,0:T(8,128)(2,1)}, u32[]{:S(2)}) copy-start(bf16[2,1,1,32,2560]{4,3,2,1,0:T(8,128)(2,1)} %constant_dynamic-slice_fusion.5) | copy-start | bytes 983044
  15.6 30.3 %copy-start.1 = (bf16[1,2560,256]{2,1,0:T(8,128)(2,1)S(1)}, bf16[1,2560,256]{2,1,0:T(8,128)(2,1)}, u32[]{:S(2)}) copy-start(bf16[1,2560,256]{2,1,0:T(8,128)(2,1)} %param.9) | copy-start | bytes 3932164
  15.7 23.1 %collective-permute-start.4 = (bf16[64,512]{1,0:T(8,128)(2,1)S(1)}, bf16[64,512]{1,0:T(8,128)(2,1)S(1)}, u32[]{:S(2)}, u32[]{:S(2)}) collective-permute-start(bf16[64,512]{1,0:T(8,128)(2,1)S(1)} %pad_maximum_fusion.6), channel_id=1, source_target_pairs={{0,8},{1,9},{2,10},{3,11},{4,12},{5,13},{6,14},{7,15},{8,16},{9,17... | collective-permute-start | bytes 196616 | tf_op jit(solution)/shard_map/ppermute | solution.py:21
  21.8 22.4 %collective-permute-start.1 = (bf16[64,2816]{1,0:T(8,128)(2,1)S(1)}, bf16[64,2816]{1,0:T(8,128)(2,1)}, u32[]{:S(2)}, u32[]{:S(2)}) collective-permute-start(bf16[64,2816]{1,0:T(8,128)(2,1)S(1)} %pad_maximum_fusion.2.own_ref), channel_id=1, source_target_pairs={{0,4},{1,5},{2,6},{3,7},{4,0},{5,1},{6,2},{7,3},{8,12},{9,13},{10,... | collective-permute-start | bytes 1081352 | tf_op jit(solution)/shard_map/ppermute | solution.py:21
  39.5 0.7 copy-start.2
  40.2 12.2 %collective-permute-start.5 = (bf16[64,2816]{1,0:T(8,128)(2,1)}, bf16[64,2816]{1,0:T(8,128)(2,1)S(1)}, u32[]{:S(2)}, u32[]{:S(2)}) collective-permute-start(bf16[64,2816]{1,0:T(8,128)(2,1)} %pad_maximum_fusion.3), channel_id=1, source_target_pairs={{0,4},{1,5},{2,6},{3,7},{4,0},{5,1},{6,2},{7,3},{8,12},{9,13},{10,... | collective-permute-start | bytes 1081352 | tf_op jit(solution)/shard_map/ppermute | solution.py:21
  45.9 6.5 %copy-start.3 = (bf16[64,2560]{1,0:T(8,128)(2,1)S(1)}, bf16[64,2560]{1,0:T(8,128)(2,1)}, u32[]{:S(2)}) copy-start(bf16[64,2560]{1,0:T(8,128)(2,1)} %copy-done.2) | copy-start | bytes 983044
  52.5 8.7 %copy-start.5 = (bf16[2,1,1,32,2560]{4,3,2,1,0:T(8,128)(2,1)S(1)}, bf16[2,1,1,32,2560]{4,3,2,1,0:T(8,128)(2,1)}, u32[]{:S(2)}) copy-start(bf16[2,1,1,32,2560]{4,3,2,1,0:T(8,128)(2,1)} %constant_dynamic-slice_fusion.5) | copy-start | bytes 983044
  55.3 12.5 %collective-permute-start.6 = (bf16[64,2560]{1,0:T(8,128)(2,1)S(1)}, bf16[64,2560]{1,0:T(8,128)(2,1)S(1)}, u32[]{:S(2)}, u32[]{:S(2)}) collective-permute-start(bf16[64,2560]{1,0:T(8,128)(2,1)S(1)} %get-tuple-element.23), channel_id=1, source_target_pairs={{0,4},{1,5},{2,6},{3,7},{4,0},{5,1},{6,2},{7,3},{8,12},{9,13},{10,... | collective-permute-start | bytes 983048 | tf_op jit(solution)/shard_map/ppermute | solution.py:21
  58.9 20.8 %collective-permute-start.7 = (bf16[64,2560]{1,0:T(8,128)(2,1)S(1)}, bf16[64,2560]{1,0:T(8,128)(2,1)S(1)}, u32[]{:S(2)}, u32[]{:S(2)}) collective-permute-start(bf16[64,2560]{1,0:T(8,128)(2,1)S(1)} %get-tuple-element.24), channel_id=1, source_target_pairs={{0,4},{1,5},{2,6},{3,7},{4,0},{5,1},{6,2},{7,3},{8,12},{9,13},{10,... | collective-permute-start | bytes 983048 | tf_op jit(solution)/shard_map/ppermute | solution.py:21
  61.7 31.0 %collective-permute-start.11 = (bf16[2560,256]{1,0:T(8,128)(2,1)S(1)}, bf16[2560,256]{1,0:T(8,128)(2,1)S(1)}, u32[]{:S(2)}, u32[]{:S(2)}) collective-permute-start(bf16[2560,256]{1,0:T(8,128)(2,1)S(1)} %fusion.2), channel_id=1, source_target_pairs={{0,1},{1,0},{2,3},{3,2},{4,5},{5,4},{6,7},{7,6},{8,9},{9,8},{10,11... | collective-permute-start | bytes 3932168 | tf_op jit(solution)/shard_map/ppermute | solution.py:21
  67.9 16.6 %collective-permute-start.9 = (bf16[32,2560]{1,0:T(8,128)(2,1)S(1)}, bf16[32,2560]{1,0:T(8,128)(2,1)S(1)}, u32[]{:S(2)}, u32[]{:S(2)}) collective-permute-start(bf16[32,2560]{1,0:T(8,128)(2,1)S(1)} %fusion.7), channel_id=1, source_target_pairs={{0,2},{1,3},{2,0},{3,1},{4,6},{5,7},{6,4},{7,5},{8,10},{9,11},{10,... | collective-permute-start | bytes 491528 | tf_op jit(solution)/shard_map/ppermute | solution.py:21
  79.9 12.8 %collective-permute-start.8 = (bf16[32,2560]{1,0:T(8,128)(2,1)S(1)}, bf16[32,2560]{1,0:T(8,128)(2,1)S(1)}, u32[]{:S(2)}, u32[]{:S(2)}) collective-permute-start(bf16[32,2560]{1,0:T(8,128)(2,1)S(1)} %fusion.6), channel_id=1, source_target_pairs={{0,2},{1,3},{2,0},{3,1},{4,6},{5,7},{6,4},{7,5},{8,10},{9,11},{10,... | collective-permute-start | bytes 491528 | tf_op jit(solution)/shard_map/ppermute | solution.py:21
  84.6 13.6 %collective-permute-start.10 = (bf16[32,2560]{1,0:T(8,128)(2,1)S(1)}, bf16[32,2560]{1,0:T(8,128)(2,1)S(1)}, u32[]{:S(2)}, u32[]{:S(2)}) collective-permute-start(bf16[32,2560]{1,0:T(8,128)(2,1)S(1)} %fusion.4), channel_id=1, source_target_pairs={{0,1016},{1,1017},{2,1018},{3,1019},{4,1020},{5,1021},{6,1022},{7,... | collective-permute-start | bytes 491528 | tf_op jit(solution)/shard_map/ppermute | solution.py:21

commit v3 on v2

--- a/solution.py
+++ b/solution.py
@@ -23,6 +23,40 @@
 
 def pick(array, index, axis):
     return lax.dynamic_index_in_dim(array, index, axis, keepdims=False)
+
+
+def gate_kernel(len_ref, gate_ref, out_ref, column_ref):
+    count = gate_ref.shape[1]
+    cap = count // 8
+    core = lax.rem(lax.axis_index("local"), 2)
+    shape = (count, count)
+    diagonal = lax.broadcasted_iota(jnp.int32, shape, 0) == lax.broadcasted_iota(jnp.int32, shape, 1)
+    gate = jnp.broadcast_to(gate_ref[...].astype(F32), shape)
+    column = jnp.sum(jnp.where(diagonal, gate, 0.0), axis=1, keepdims=True)
+    column_ref[...] = jnp.broadcast_to(column, column_ref.shape)
+    slot = lax.broadcasted_iota(jnp.int32, (cap, out_ref.shape[1]), 0)
+    for chip in range(2):
+        for k in range(2):
+            block = (2 * chip + core) * 2 + k
+            gates = column_ref[pl.ds(pl.multiple_of(block * cap, cap), cap), :]
+            first = (2 * chip + k) * cap
+            out_ref[first : first + cap, :] = jnp.where(slot < len_ref[block], gates, 0.0)
+
+
+def live_gates(lengths, gates, wide):
+    count = gates.shape[1]
+    vmem = pl.BlockSpec(memory_space=pltpu.VMEM)
+    return pl.pallas_call(
+        gate_kernel,
+        out_shape=jax.ShapeDtypeStruct((count // 2, wide), F32),
+        in_specs=[pl.BlockSpec(memory_space=pltpu.SMEM), vmem],
+        out_specs=vmem,
+        scratch_shapes=[pltpu.VMEM((count, wide), F32)],
+        compiler_params=pltpu.CompilerParams(vmem_limit_bytes=4 * 1024 * 1024),
+        cost_estimate=pl.CostEstimate(
+            flops=8 * count * count, bytes_accessed=64 * 1024 * 1024, transcendentals=0
+        ),
+    )(lengths, gates)
 
 
 def expert_kernel(own_ref, own_cot_ref, got_ref, got_cot_ref, own_w_ref, other_w_ref, dh_ref, give_ref, keep_ref):
@@ -70,9 +104,9 @@
         ),
         in_specs=[vmem] * 6,
         out_specs=(vmem,) * 3,
-        compiler_params=pltpu.CompilerParams(vmem_limit_bytes=32 * 1024 * 1024),
+        compiler_params=pltpu.CompilerParams(vmem_limit_bytes=12 * 1024 * 1024),
         cost_estimate=pl.CostEstimate(
-            flops=8 * half * dim * wide * 2, bytes_accessed=8 * 1024 * 1024, transcendentals=2 * half * wide
+            flops=16 * half * dim * wide, bytes_accessed=4 * 1024 * 1024, transcendentals=2 * half * wide
         ),
     )(own, own_cot, got, got_cot, own_w, other_w)
 
@@ -112,15 +146,15 @@
     act_mine = pick(acts, core, 1)
     lengths = pick(group_len, node, 0)
     alive = jnp.arange(cap)[None, None, :] < lengths[:, :, None]
-    gates = jnp.where(alive.reshape(node_rows), slot_gate, jnp.zeros_like(slot_gate))
-    gates = pick(gates.reshape(far_count, 2, 2, cap), core, 1).astype(F32)
+    gates = live_gates(lengths.reshape(-1), slot_gate.reshape(1, node_rows), 2 * width)
+    gates = gates.reshape(far_count, 2, cap, 2 * width)
 
     def cots(which):
         cut_to = [
             pick(a.reshape(far_count, 2, cap, 2, width), which, 3) for a in (act_mine, act_other)
         ]
         both = jnp.concatenate(cut_to, axis=-1).astype(F32)
-        return (both * gates[..., None]).astype(BF)
+        return (both * gates).astype(BF)
 
     def group(array, k):
         return array[:, k].reshape(half, array.shape[-1])

time: 99.7 us -> 99.7 us (level)
    unnamed x18 -> x20, local copies, waits for them, and re-layouts: 2.96 us -> 2.95 us
  transfers between devices with their start and end apart: 12 -> 12, of which waited for: 5 -> 5; matrix products, arithmetic and copies ran while one was open for 8% -> 8% of each run, Pallas kernels for 3% -> 4%
where the time goes in v3:
time: 99.7 us; the launch traced here: 99 us
  starting transfers between devices  53 us (53%)
  waiting for transfers between devices  26.4 us (26%)
  local copies, waits for them, and re-layouts  7.95 us (8%)
  Pallas kernels  6.32 us (6%)
  matrix products  2.18 us (2%)
  other arithmetic  2.01 us (2%)
  between operations  1.1 us (1%)
    ppermute x12, starting transfers between devices, moved(): return lax.ppermute(value, ('node', 'local'), route)  53 us
    ppermute x12, waiting for transfers between devices, moved(): return lax.ppermute(value, ('node', 'local'), route)  26.4 us
    pallas_call x2, Pallas kernels, expert_work(): pl.pallas_call(expert_kernel, out_shape=(jax.ShapeDtypeStruct((2 * half,...  5.66 us
    unnamed x20, local copies, waits for them, and re-layouts  2.95 us
    dot_general x2, matrix products, weight_grads(): lax.dot_general(rows, dh, (((0,), (0,)), ((), ())), preferred_element_typ...  2.18 us
  transfers between devices with their start and end apart: 12, of which 5 were waited for; matrix products, arithmetic and copies ran while one was open for 8% of the time, Pallas kernels for 4%

profile of v3, /device:TPU:14, one launch (start us, length us, event | category | flops | bytes accessed | tf_op | source)
XLA Modules:
  0.0 99.0 jit_solution(8197268500377767535)
XLA Ops:
  0.6 0.0 copy-start
  0.7 1.3 %copy-done = bf16[256,2560]{1,0:T(8,128)(2,1)S(1)} copy-done((bf16[256,2560]{1,0:T(8,128)(2,1)S(1)}, bf16[256,2560]{1,0:T(8,128)(2,1)}, u32[]{:S(2)}) %copy-start) | copy-done | bytes 1310744
  2.0 0.7 constant_dynamic-slice_fusion.5
  2.7 0.9 dynamic-slice_bitcast_fusion.1
  3.6 1.9 %collective-permute-start = (bf16[2,2,32,256]{3,2,1,0:T(8,128)(2,1)S(1)}, bf16[2,2,32,256]{3,2,1,0:T(8,128)(2,1)S(1)}, u32[]{:S(2)}, u32[]{:S(2)}) collective-permute-start(bf16[2,2,32,256]{3,2,1,0:T(8,128)(2,1)S(1)} %get-tuple-element.35), channel_id=1, source_target_pairs={{0,1},{1,0},{2,3},{3,2},{4,5},{5,4},{6,7},{7,6},{8,9},{9,8},{10,11... | collective-permute-start | bytes 196616 | tf_op jit(solution)/shard_map/ppermute | solution.py:21
  5.5 4.7 %collective-permute-start.3 = (bf16[64,2560]{1,0:T(8,128)(2,1)}, bf16[64,2560]{1,0:T(8,128)(2,1)S(1)}, u32[]{:S(2)}, u32[]{:S(2)}) collective-permute-start(bf16[64,2560]{1,0:T(8,128)(2,1)} %bitcast.2), channel_id=1, source_target_pairs={{0,8},{1,9},{2,10},{3,11},{4,12},{5,13},{6,14},{7,15},{8,16},{9,17... | collective-permute-start | bytes 983048 | tf_op jit(solution)/shard_map/ppermute | solution.py:21
  10.2 2.1 %collective-permute-start.2 = (bf16[2560,256]{1,0:T(8,128)(2,1)}, bf16[2560,256]{1,0:T(8,128)(2,1)}, u32[]{:S(2)}, u32[]{:S(2)}) collective-permute-start(bf16[2560,256]{1,0:T(8,128)(2,1)} %bitcast.65), channel_id=1, source_target_pairs={{0,1},{1,0},{2,3},{3,2},{4,5},{5,4},{6,7},{7,6},{8,9},{9,8},{10,11... | collective-permute-start | bytes 3932168 | tf_op jit(solution)/shard_map/ppermute | solution.py:21
  12.4 0.7 reshape.62.gate_ref
  13.1 0.8 constant_dynamic-slice_fusion.4
  13.9 0.2 fusion.12
  14.1 0.1 reshape.61.len_ref
  14.2 0.1 copy.20
  14.3 0.1 copy.21
  14.4 0.7 shard_map.68
  15.1 0.0 collective-permute-done
  15.1 0.3 constant_dynamic-slice_fusion.2
  15.6 0.0 copy-start.1
  15.6 6.1 %collective-permute-start.4 = (bf16[64,512]{1,0:T(8,128)(2,1)S(1)}, bf16[64,512]{1,0:T(8,128)(2,1)S(1)}, u32[]{:S(2)}, u32[]{:S(2)}) collective-permute-start(bf16[64,512]{1,0:T(8,128)(2,1)S(1)} %pad_maximum_fusion.6), channel_id=1, source_target_pairs={{0,8},{1,9},{2,10},{3,11},{4,12},{5,13},{6,14},{7,15},{8,16},{9,17... | collective-permute-start | bytes 196616 | tf_op jit(solution)/shard_map/ppermute | solution.py:21
  21.7 2.7 %collective-permute-start.1 = (bf16[64,2816]{1,0:T(8,128)(2,1)S(1)}, bf16[64,2816]{1,0:T(8,128)(2,1)}, u32[]{:S(2)}, u32[]{:S(2)}) collective-permute-start(bf16[64,2816]{1,0:T(8,128)(2,1)S(1)} %pad_maximum_fusion.2.own_ref), channel_id=1, source_target_pairs={{0,4},{1,5},{2,6},{3,7},{4,0},{5,1},{6,2},{7,3},{8,12},{9,13},{10,... | collective-permute-start | bytes 1081352 | tf_op jit(solution)/shard_map/ppermute | solution.py:21
  24.4 14.3 %collective-permute-done.4 = bf16[64,512]{1,0:T(8,128)(2,1)S(1)} collective-permute-done((bf16[64,512]{1,0:T(8,128)(2,1)S(1)}, bf16[64,512]{1,0:T(8,128)(2,1)S(1)}, u32[]{:S(2)}, u32[]{:S(2)}) %collective-permute-start.4) | collective-permute-done | bytes 65568 | tf_op jit(solution)/shard_map/ppermute | solution.py:21
  38.7 0.8 pad_maximum_fusion.3
  39.5 0.7 copy-done.2
  40.2 3.8 %collective-permute-start.5 = (bf16[64,2816]{1,0:T(8,128)(2,1)}, bf16[64,2816]{1,0:T(8,128)(2,1)S(1)}, u32[]{:S(2)}, u32[]{:S(2)}) collective-permute-start(bf16[64,2816]{1,0:T(8,128)(2,1)} %pad_maximum_fusion.3), channel_id=1, source_target_pairs={{0,4},{1,5},{2,6},{3,7},{4,0},{5,1},{6,2},{7,3},{8,12},{9,13},{10,... | collective-permute-start | bytes 1081352 | tf_op jit(solution)/shard_map/ppermute | solution.py:21
  44.0 0.1 iota_compare_fusion
  44.1 0.1 broadcast_in_dim.19
  44.2 0.0 collective-permute-done.1.got_ref
  44.2 0.8 slice.50.got_cot_ref
  45.0 1.0 %slice.55 = bf16[64,2560]{1,0:T(8,128)(2,1)S(1)} slice(bf16[64,2816]{1,0:T(8,128)(2,1)} %collective-permute-done.1.got_ref), slice={[0:64], [0:2560]} | slice | bytes 655360 | tf_op jit(solution)/shard_map/slice | solution.py:176
  46.0 0.0 copy-start.3
  46.0 2.9 %shard_map.69 = (bf16[128,512]{1,0:T(8,128)(2,1)S(1)}, bf16[64,2560]{1,0:T(8,128)(2,1)S(1)}, f32[64,2560]{1,0:T(8,128)S(1)}) custom-call(bf16[64,2816]{1,0:T(8,128)(2,1)S(1)} %pad_maximum_fusion.2.own_ref, bf16[64,256]{1,0:T(8,128)(2,1)S(1)} %bitcast.69, bf16[64,2816]{1,0:T(8,128)(2,1)} %collective-permute-done.1.got_ref, ...), custom_call_target="tpu_custom_call" | custom-call | flops 671088640 | bytes 4194304 | tf_op jit(solution)/shard_map/pallas_call | solution.py:98
  48.9 3.5 %collective-permute-done.5.got_ref = bf16[64,2816]{1,0:T(8,128)(2,1)S(1)} collective-permute-done((bf16[64,2816]{1,0:T(8,128)(2,1)}, bf16[64,2816]{1,0:T(8,128)(2,1)S(1)}, u32[]{:S(2)}, u32[]{:S(2)}) %collective-permute-start.5) | collective-permute-done | bytes 360480 | tf_op jit(solution)/shard_map/ppermute | solution.py:21
  52.5 2.8 %shard_map.70 = (bf16[128,512]{1,0:T(8,128)(2,1)S(1)}, bf16[64,2560]{1,0:T(8,128)(2,1)S(1)}, f32[64,2560]{1,0:T(8,128)S(1)}) custom-call(bf16[64,2560]{1,0:T(8,128)(2,1)S(1)} %copy-done.3, bf16[64,256]{1,0:T(8,128)(2,1)S(1)} %get-tuple-element.41.own_cot_ref, bf16[64,2816]{1,0:T(8,128)(2,1)S(1)} %collective-permute-done.5.got_ref, ...), custom_call_target="tpu_custom_call" | custom-call | flops 671088640 | bytes 4194304 | tf_op jit(solution)/shard_map/pallas_call | solution.py:98
  55.3 3.6 %collective-permute-start.6 = (bf16[64,2560]{1,0:T(8,128)(2,1)S(1)}, bf16[64,2560]{1,0:T(8,128)(2,1)S(1)}, u32[]{:S(2)}, u32[]{:S(2)}) collective-permute-start(bf16[64,2560]{1,0:T(8,128)(2,1)S(1)} %get-tuple-element.23), channel_id=1, source_target_pairs={{0,4},{1,5},{2,6},{3,7},{4,0},{5,1},{6,2},{7,3},{8,12},{9,13},{10,... | collective-permute-start | bytes 983048 | tf_op jit(solution)/shard_map/ppermute | solution.py:21
  58.9 2.2 %collective-permute-start.7 = (bf16[64,2560]{1,0:T(8,128)(2,1)S(1)}, bf16[64,2560]{1,0:T(8,128)(2,1)S(1)}, u32[]{:S(2)}, u32[]{:S(2)}) collective-permute-start(bf16[64,2560]{1,0:T(8,128)(2,1)S(1)} %get-tuple-element.24), channel_id=1, source_target_pairs={{0,4},{1,5},{2,6},{3,7},{4,0},{5,1},{6,2},{7,3},{8,12},{9,13},{10,... | collective-permute-start | bytes 983048 | tf_op jit(solution)/shard_map/ppermute | solution.py:21
  61.1 0.6 fusion.2
  61.7 1.9 %collective-permute-start.11 = (bf16[2560,256]{1,0:T(8,128)(2,1)S(1)}, bf16[2560,256]{1,0:T(8,128)(2,1)S(1)}, u32[]{:S(2)}, u32[]{:S(2)}) collective-permute-start(bf16[2560,256]{1,0:T(8,128)(2,1)S(1)} %fusion.2), channel_id=1, source_target_pairs={{0,1},{1,0},{2,3},{3,2},{4,5},{5,4},{6,7},{7,6},{8,9},{9,8},{10,11... | collective-permute-start | bytes 3932168 | tf_op jit(solution)/shard_map/ppermute | solution.py:21
  63.6 4.2 %collective-permute-done.6 = bf16[64,2560]{1,0:T(8,128)(2,1)S(1)} collective-permute-done((bf16[64,2560]{1,0:T(8,128)(2,1)S(1)}, bf16[64,2560]{1,0:T(8,128)(2,1)S(1)}, u32[]{:S(2)}, u32[]{:S(2)}) %collective-permute-start.6) | collective-permute-done | bytes 327712 | tf_op jit(solution)/shard_map/ppermute | solution.py:21
  67.8 0.1 convert_add_fusion.1
  67.9 11.9 %collective-permute-start.9 = (bf16[32,2560]{1,0:T(8,128)(2,1)S(1)}, bf16[32,2560]{1,0:T(8,128)(2,1)S(1)}, u32[]{:S(2)}, u32[]{:S(2)}) collective-permute-start(bf16[32,2560]{1,0:T(8,128)(2,1)S(1)} %fusion.7), channel_id=1, source_target_pairs={{0,2},{1,3},{2,0},{3,1},{4,6},{5,7},{6,4},{7,5},{8,10},{9,11},{10,... | collective-permute-start | bytes 491528 | tf_op jit(solution)/shard_map/ppermute | solution.py:21
  79.8 0.0 collective-permute-done.7
  79.8 0.1 convert_add_fusion
  79.9 4.6 %collective-permute-start.8 = (bf16[32,2560]{1,0:T(8,128)(2,1)S(1)}, bf16[32,2560]{1,0:T(8,128)(2,1)S(1)}, u32[]{:S(2)}, u32[]{:S(2)}) collective-permute-start(bf16[32,2560]{1,0:T(8,128)(2,1)S(1)} %fusion.6), channel_id=1, source_target_pairs={{0,2},{1,3},{2,0},{3,1},{4,6},{5,7},{6,4},{7,5},{8,10},{9,11},{10,... | collective-permute-start | bytes 491528 | tf_op jit(solution)/shard_map/ppermute | solution.py:21
  84.5 0.5 collective-permute-done.9
  85.1 7.4 %collective-permute-start.10 = (bf16[32,2560]{1,0:T(8,128)(2,1)S(1)}, bf16[32,2560]{1,0:T(8,128)(2,1)S(1)}, u32[]{:S(2)}, u32[]{:S(2)}) collective-permute-start(bf16[32,2560]{1,0:T(8,128)(2,1)S(1)} %fusion.4), channel_id=1, source_target_pairs={{0,1016},{1,1017},{2,1018},{3,1019},{4,1020},{5,1021},{6,1022},{7,... | collective-permute-start | bytes 491528 | tf_op jit(solution)/shard_map/ppermute | solution.py:21
  92.6 0.0 collective-permute-done.8
  92.6 1.6 %fusion.1 = bf16[2560,256]{1,0:T(8,128)(2,1)} fusion(bf16[2560,256]{1,0:T(8,128)(2,1)S(1)} %collective-permute-done.11, bf16[64,2560]{1,0:T(8,128)(2,1)S(1)} %slice.45, bf16[64,2560]{1,0:T(8,128)(2,1)S(1)} %copy-done.3, bf16[64,2560]{1,0:T(8,128)(2,1)S(1)} %slice.55, bf16[64,2560]{1,0:T(8,128)(2,1)S(1)} %bitcast.76, ...), kind=kOutput, calls=%fused_computation.3 | convolution fusion | flops 343408640 | bytes 4063232 | tf_op jit(solution)/shard_map/dot_general | solution.py:115
  94.2 3.9 %collective-permute-done.10 = bf16[32,2560]{1,0:T(8,128)(2,1)S(1)} collective-permute-done((bf16[32,2560]{1,0:T(8,128)(2,1)S(1)}, bf16[32,2560]{1,0:T(8,128)(2,1)S(1)}, u32[]{:S(2)}, u32[]{:S(2)}) %collective-permute-start.10) | collective-permute-done | bytes 163872 | tf_op jit(solution)/shard_map/ppermute | solution.py:21
  98.1 0.9 fusion.3
  (34 shorter events, 0.4 us)
Async XLA Ops:
  0.6 1.3 %copy-start = (bf16[256,2560]{1,0:T(8,128)(2,1)S(1)}, bf16[256,2560]{1,0:T(8,128)(2,1)}, u32[]{:S(2)}) copy-start(bf16[256,2560]{1,0:T(8,128)(2,1)} %param.5) | copy-start | bytes 3932164
  0.6 13.2 %copy-start.6 = (s32[256,4,2]{0,2,1:T(2,128)S(1)}, s32[256,4,2]{0,2,1:T(2,128)}, u32[]{:S(2)}) copy-start(s32[256,4,2]{0,2,1:T(2,128)} %param.6) | copy-start | bytes 24580
  3.6 11.5 %collective-permute-start = (bf16[2,2,32,256]{3,2,1,0:T(8,128)(2,1)S(1)}, bf16[2,2,32,256]{3,2,1,0:T(8,128)(2,1)S(1)}, u32[]{:S(2)}, u32[]{:S(2)}) collective-permute-start(bf16[2,2,32,256]{3,2,1,0:T(8,128)(2,1)S(1)} %get-tuple-element.35), channel_id=1, source_target_pairs={{0,1},{1,0},{2,3},{3,2},{4,5},{5,4},{6,7},{7,6},{8,9},{9,8},{10,11... | collective-permute-start | bytes 196616 | tf_op jit(solution)/shard_map/ppermute | solution.py:21
  5.5 33.2 %collective-permute-start.3 = (bf16[64,2560]{1,0:T(8,128)(2,1)}, bf16[64,2560]{1,0:T(8,128)(2,1)S(1)}, u32[]{:S(2)}, u32[]{:S(2)}) collective-permute-start(bf16[64,2560]{1,0:T(8,128)(2,1)} %bitcast.2), channel_id=1, source_target_pairs={{0,8},{1,9},{2,10},{3,11},{4,12},{5,13},{6,14},{7,15},{8,16},{9,17... | collective-permute-start | bytes 983048 | tf_op jit(solution)/shard_map/ppermute | solution.py:21
  10.2 35.7 %collective-permute-start.2 = (bf16[2560,256]{1,0:T(8,128)(2,1)}, bf16[2560,256]{1,0:T(8,128)(2,1)}, u32[]{:S(2)}, u32[]{:S(2)}) collective-permute-start(bf16[2560,256]{1,0:T(8,128)(2,1)} %bitcast.65), channel_id=1, source_target_pairs={{0,1},{1,0},{2,3},{3,2},{4,5},{5,4},{6,7},{7,6},{8,9},{9,8},{10,11... | collective-permute-start | bytes 3932168 | tf_op jit(solution)/shard_map/ppermute | solution.py:21
  15.1 6.6 %copy-start.4 = (bf16[2,1,1,32,2560]{4,3,2,1,0:T(8,128)(2,1)S(1)}, bf16[2,1,1,32,2560]{4,3,2,1,0:T(8,128)(2,1)}, u32[]{:S(2)}) copy-start(bf16[2,1,1,32,2560]{4,3,2,1,0:T(8,128)(2,1)} %constant_dynamic-slice_fusion.4) | copy-start | bytes 983044
  15.6 30.4 %copy-start.1 = (bf16[1,2560,256]{2,1,0:T(8,128)(2,1)S(1)}, bf16[1,2560,256]{2,1,0:T(8,128)(2,1)}, u32[]{:S(2)}) copy-start(bf16[1,2560,256]{2,1,0:T(8,128)(2,1)} %param.9) | copy-start | bytes 3932164
  15.6 23.1 %collective-permute-start.4 = (bf16[64,512]{1,0:T(8,128)(2,1)S(1)}, bf16[64,512]{1,0:T(8,128)(2,1)S(1)}, u32[]{:S(2)}, u32[]{:S(2)}) collective-permute-start(bf16[64,512]{1,0:T(8,128)(2,1)S(1)} %pad_maximum_fusion.6), channel_id=1, source_target_pairs={{0,8},{1,9},{2,10},{3,11},{4,12},{5,13},{6,14},{7,15},{8,16},{9,17... | collective-permute-start | bytes 196616 | tf_op jit(solution)/shard_map/ppermute | solution.py:21
  21.7 22.5 %collective-permute-start.1 = (bf16[64,2816]{1,0:T(8,128)(2,1)S(1)}, bf16[64,2816]{1,0:T(8,128)(2,1)}, u32[]{:S(2)}, u32[]{:S(2)}) collective-permute-start(bf16[64,2816]{1,0:T(8,128)(2,1)S(1)} %pad_maximum_fusion.2.own_ref), channel_id=1, source_target_pairs={{0,4},{1,5},{2,6},{3,7},{4,0},{5,1},{6,2},{7,3},{8,12},{9,13},{10,... | collective-permute-start | bytes 1081352 | tf_op jit(solution)/shard_map/ppermute | solution.py:21
  39.5 0.7 copy-start.2
  40.2 12.2 %collective-permute-start.5 = (bf16[64,2816]{1,0:T(8,128)(2,1)}, bf16[64,2816]{1,0:T(8,128)(2,1)S(1)}, u32[]{:S(2)}, u32[]{:S(2)}) collective-permute-start(bf16[64,2816]{1,0:T(8,128)(2,1)} %pad_maximum_fusion.3), channel_id=1, source_target_pairs={{0,4},{1,5},{2,6},{3,7},{4,0},{5,1},{6,2},{7,3},{8,12},{9,13},{10,... | collective-permute-start | bytes 1081352 | tf_op jit(solution)/shard_map/ppermute | solution.py:21
  46.0 6.5 %copy-start.3 = (bf16[64,2560]{1,0:T(8,128)(2,1)S(1)}, bf16[64,2560]{1,0:T(8,128)(2,1)}, u32[]{:S(2)}) copy-start(bf16[64,2560]{1,0:T(8,128)(2,1)} %copy-done.2) | copy-start | bytes 983044
  52.5 8.7 %copy-start.5 = (bf16[2,1,1,32,2560]{4,3,2,1,0:T(8,128)(2,1)S(1)}, bf16[2,1,1,32,2560]{4,3,2,1,0:T(8,128)(2,1)}, u32[]{:S(2)}) copy-start(bf16[2,1,1,32,2560]{4,3,2,1,0:T(8,128)(2,1)} %constant_dynamic-slice_fusion.4) | copy-start | bytes 983044
  55.3 12.5 %collective-permute-start.6 = (bf16[64,2560]{1,0:T(8,128)(2,1)S(1)}, bf16[64,2560]{1,0:T(8,128)(2,1)S(1)}, u32[]{:S(2)}, u32[]{:S(2)}) collective-permute-start(bf16[64,2560]{1,0:T(8,128)(2,1)S(1)} %get-tuple-element.23), channel_id=1, source_target_pairs={{0,4},{1,5},{2,6},{3,7},{4,0},{5,1},{6,2},{7,3},{8,12},{9,13},{10,... | collective-permute-start | bytes 983048 | tf_op jit(solution)/shard_map/ppermute | solution.py:21
  58.9 20.9 %collective-permute-start.7 = (bf16[64,2560]{1,0:T(8,128)(2,1)S(1)}, bf16[64,2560]{1,0:T(8,128)(2,1)S(1)}, u32[]{:S(2)}, u32[]{:S(2)}) collective-permute-start(bf16[64,2560]{1,0:T(8,128)(2,1)S(1)} %get-tuple-element.24), channel_id=1, source_target_pairs={{0,4},{1,5},{2,6},{3,7},{4,0},{5,1},{6,2},{7,3},{8,12},{9,13},{10,... | collective-permute-start | bytes 983048 | tf_op jit(solution)/shard_map/ppermute | solution.py:21
  61.7 30.9 %collective-permute-start.11 = (bf16[2560,256]{1,0:T(8,128)(2,1)S(1)}, bf16[2560,256]{1,0:T(8,128)(2,1)S(1)}, u32[]{:S(2)}, u32[]{:S(2)}) collective-permute-start(bf16[2560,256]{1,0:T(8,128)(2,1)S(1)} %fusion.2), channel_id=1, source_target_pairs={{0,1},{1,0},{2,3},{3,2},{4,5},{5,4},{6,7},{7,6},{8,9},{9,8},{10,11... | collective-permute-start | bytes 3932168 | tf_op jit(solution)/shard_map/ppermute | solution.py:21
  67.9 17.2 %collective-permute-start.9 = (bf16[32,2560]{1,0:T(8,128)(2,1)S(1)}, bf16[32,2560]{1,0:T(8,128)(2,1)S(1)}, u32[]{:S(2)}, u32[]{:S(2)}) collective-permute-start(bf16[32,2560]{1,0:T(8,128)(2,1)S(1)} %fusion.7), channel_id=1, source_target_pairs={{0,2},{1,3},{2,0},{3,1},{4,6},{5,7},{6,4},{7,5},{8,10},{9,11},{10,... | collective-permute-start | bytes 491528 | tf_op jit(solution)/shard_map/ppermute | solution.py:21
  79.9 12.7 %collective-permute-start.8 = (bf16[32,2560]{1,0:T(8,128)(2,1)S(1)}, bf16[32,2560]{1,0:T(8,128)(2,1)S(1)}, u32[]{:S(2)}, u32[]{:S(2)}) collective-permute-start(bf16[32,2560]{1,0:T(8,128)(2,1)S(1)} %fusion.6), channel_id=1, source_target_pairs={{0,2},{1,3},{2,0},{3,1},{4,6},{5,7},{6,4},{7,5},{8,10},{9,11},{10,... | collective-permute-start | bytes 491528 | tf_op jit(solution)/shard_map/ppermute | solution.py:21
  85.1 13.0 %collective-permute-start.10 = (bf16[32,2560]{1,0:T(8,128)(2,1)S(1)}, bf16[32,2560]{1,0:T(8,128)(2,1)S(1)}, u32[]{:S(2)}, u32[]{:S(2)}) collective-permute-start(bf16[32,2560]{1,0:T(8,128)(2,1)S(1)} %fusion.4), channel_id=1, source_target_pairs={{0,1016},{1,1017},{2,1018},{3,1019},{4,1020},{5,1021},{6,1022},{7,... | collective-permute-start | bytes 491528 | tf_op jit(solution)/shard_map/ppermute | solution.py:21
